TPU v7x, 256 devices: a whole 4x4x8 slice. The times are simulated.
256 devices in a mesh: ctx: 64 (over z, y, x_lo), tp: 4 (over x_hi, core).
Axes of the slice: x: 4 (x_hi: 2, x_lo: 2; x = x_hi * 2 + x_lo), y: 4, z: 8, core: 2. Of those that a mesh axis runs over, the one named last changes fastest.
Arguments:
- block_input: bfloat16 [8192, 4096], P(('ctx', 'tp')), may hold values from -6 to 6
- featurizer: bfloat16 [4096, 3, 2048], P('ctx', None, 'tp'), may hold values from -0.09375 to 0.09375
- filters: bfloat16 [2048, 128], P('tp'), may hold values from -0.5 to 0.5
- out_weight: bfloat16 [4096, 2048], P('ctx', 'tp'), may hold values from -0.125 to 0.125
- grad_output: bfloat16 [8192, 4096], P(('ctx', 'tp')), may hold values from -24 to 24
Outputs:
- grad_features: bfloat16 [8192, 3, 2048], P('ctx', None, 'tp')
- grad_out_weight: float32 [4096, 2048], P('ctx', 'tp')
- grad_filters: float32 [2048, 128], P('tp')
All inputs are finite; a program needn't handle non-finite values.
Results may differ from a plain program's by a relative error of at most 0.015.
Values may be sent and summed in bfloat16 or wider, within the bound.
A program may use at most 128 MiB of HBM per device.

v0:
```python
import math

import jax
import jax.numpy as jnp
from jax import lax
from jax.sharding import PartitionSpec as P


def shifted(value, axis, by):
    length = lax.axis_size(axis)
    pairs = [(i, i + by) for i in range(length) if 0 <= i + by < length]
    return lax.ppermute(value, axis, pairs)


def skew_taps(taps_part):
    width_group, ntaps = taps_part.shape
    zero_first = jnp.zeros((width_group, 1), taps_part.dtype)
    zero_rest = jnp.zeros((width_group, ntaps), taps_part.dtype)
    base_row = jnp.concatenate([zero_first, taps_part[:, ::-1], zero_rest], axis=1)
    tiled = jnp.broadcast_to(base_row[:, None, :], (width_group, ntaps, 2 * ntaps + 1))
    flat = tiled.reshape(width_group, ntaps * (2 * ntaps + 1))[:, : 2 * ntaps * ntaps]
    return flat.reshape(width_group, ntaps, 2 * ntaps)


def block_windows(extended, ntaps):
    count_blocks = extended.shape[0] // ntaps - 1
    blocks = extended.reshape(count_blocks + 1, ntaps, extended.shape[1])
    return jnp.concatenate([blocks[:-1], blocks[1:]], axis=1)


def split_groups(values, ngroups, group):
    return values.reshape(values.shape[0], ngroups, group).transpose(1, 0, 2)


def join_groups(values):
    return values.transpose(1, 0, 2).reshape(values.shape[1], values.shape[0] * values.shape[2])


def on_device(block_input, featurizer, filters, out_weight, grad_output):
    ntaps = filters.shape[1]
    width_local = filters.shape[0]
    input_slab = lax.all_gather(block_input, "tp", axis=0, tiled=True)
    grad_slab = lax.all_gather(grad_output, "tp", axis=0, tiled=True)
    slab = input_slab.shape[0]
    piece_rows = lax.all_gather(featurizer, "ctx", axis=0, tiled=True)
    columns = input_slab
    flat_piece = piece_rows.reshape(piece_rows.shape[0], 3 * width_local)
    projected = jnp.dot(columns, flat_piece, preferred_element_type=jnp.float32)
    columns = grad_slab
    grad_mixer_sum = jnp.dot(
        columns,
        lax.all_gather(out_weight, "ctx", axis=0, tiled=True),
        preferred_element_type=jnp.float32,
    )
    features = projected.astype(jnp.bfloat16).reshape(slab, 3, width_local)
    query_rows = features[:, 0].astype(jnp.float32)
    key_rows = features[:, 1].astype(jnp.float32)
    value_rows = features[:, 2].astype(jnp.float32)
    gated = (key_rows * value_rows).astype(jnp.bfloat16)
    history = shifted(gated, "ctx", 1)
    grad_mixer_f = grad_mixer_sum.astype(jnp.bfloat16).astype(jnp.float32)
    grad_mixed = (grad_mixer_f * query_rows).astype(jnp.bfloat16)
    future = shifted(grad_mixed, "ctx", -1)
    group = 128
    ngroups = width_local // group
    gated_ext = jnp.concatenate([history, gated], axis=0)
    reversed_ext = jnp.concatenate([future[::-1], grad_mixed[::-1]], axis=0)
    tap_groups = filters.reshape(ngroups, group, ntaps)
    count_blocks = slab // ntaps

    def one_group(group_items):
        gated_part, reversed_part, forward_part, taps_part = group_items
        toeplitz = skew_taps(taps_part)
        gated_windows = block_windows(gated_part, ntaps)
        reversed_windows = block_windows(reversed_part, ntaps)
        mixed_part = jnp.einsum(
            "ciw,bwc->bic", toeplitz, gated_windows, preferred_element_type=jnp.float32
        ).reshape(slab, group)
        back_part = jnp.einsum(
            "ciw,bwc->bic", toeplitz, reversed_windows, preferred_element_type=jnp.float32
        ).reshape(slab, group)
        forward_blocks = forward_part.reshape(count_blocks, ntaps, group)
        correl = jnp.einsum(
            "bic,bwc->ciw", forward_blocks, gated_windows, preferred_element_type=jnp.float32
        )
        flat_corr = jnp.pad(correl.reshape(group, 2 * ntaps * ntaps), ((0, 0), (0, ntaps)))
        banded = flat_corr.reshape(group, ntaps, 2 * ntaps + 1)[:, :, 1 : ntaps + 1]
        tap_terms = jnp.sum(banded, axis=1)[:, ::-1]
        return (mixed_part, back_part, tap_terms)

    mixed_groups, back_groups, tap_groups_out = lax.map(
        one_group,
        (
            split_groups(gated_ext, ngroups, group),
            split_groups(reversed_ext, ngroups, group),
            split_groups(grad_mixed, ngroups, group),
            tap_groups,
        ),
    )
    mixed = join_groups(mixed_groups)
    grad_gated = join_groups(back_groups)[::-1]
    filter_terms = tap_groups_out.reshape(width_local, ntaps)
    mixer_out = (query_rows * mixed).astype(jnp.bfloat16)
    grad_features = jnp.stack(
        [grad_mixer_f * mixed, grad_gated * value_rows, grad_gated * key_rows], axis=1
    ).astype(jnp.bfloat16)
    scale_factor = 1.0 / math.sqrt(slab * lax.axis_size("ctx"))
    columns = grad_slab
    weight_sum = lax.psum_scatter(
        lax.dot_general(
            columns, mixer_out, (((0,), (0,)), ((), ())), preferred_element_type=jnp.float32
        ),
        "ctx",
        scatter_dimension=0,
        tiled=True,
    )
    filter_sum = lax.psum(filter_terms, "ctx")
    return (grad_features, weight_sum * scale_factor, filter_sum * scale_factor)


def solution(mesh):
    placed = (
        P(("ctx", "tp"), None),
        P("ctx", None, "tp"),
        P("tp", None),
        P("ctx", "tp"),
        P(("ctx", "tp"), None),
    )
    return jax.shard_map(
        on_device,
        mesh=mesh,
        in_specs=placed,
        out_specs=(P("ctx", None, "tp"), P("ctx", "tp"), P("tp", None)),
        check_vma=False,
    )
```

profile of v0, /device:TPU:4, one launch (start us, length us, event | category | flops | bytes accessed | tf_op | source)
XLA Modules:
  0.0 1829.7 jit_solution(5637243495869659642)
XLA Ops:
  7.2 0.7 all-gather.11.cloned.1.call-update
  7.9 0.7 all-gather.9.cloned.1.call-update
  8.7 0.7 all-gather.5.cloned.1.call-update
  9.4 0.5 all-gather.7.cloned.1.call-update
  10.0 329.4 %all-gather.11.cloned.1.call-done = bf16[4096,3,512]{2,0,1:T(8,128)(2,1)} async-done(((bf16[64,3,512]{2,0,1:T(8,128)(2,1)}), bf16[4096,3,512]{2,0,1:T(8,128)(2,1)}) %all-gather.11.cloned.1.call-update) | async-done | bytes 12582928 | tf_op jit(solution)/shard_map/all_gather | solution.py:45
  339.4 17.0 copy.39
  356.4 2.4 all-gather.9.cloned.1.call-done
  358.8 9.2 convolution_convert_fusion
  368.0 0.2 copy.40
  368.3 15.0 all-gather.5.cloned.1.call-done
  383.4 308.4 %all-gather.7.cloned.1.call-done = bf16[4096,512]{1,0:T(8,128)(2,1)} async-done(((bf16[64,512]{1,0:T(8,128)(2,1)}), bf16[4096,512]{1,0:T(8,128)(2,1)}) %all-gather.7.cloned.1.call-update) | async-done | bytes 4194320 | tf_op jit(solution)/shard_map/all_gather | solution.py:52
  691.8 3.9 fusion.6
  695.7 1.3 collective-permute-start.1
  697.3 4.6 collective-permute-start
  701.9 0.2 rev.22
  702.1 0.5 collective-permute-done.1
  702.6 0.2 rev.21
  702.8 1.6 collective-permute-done
  704.5 224.8 %while.16 = (s32[]{:T(128)}, f32[4,128,128]{2,1,0:T(8,128)S(1)}, f32[4,128,128]{2,1,0:T(8,128)S(1)}, f32[4,128,128]{2,1,0:T(8,128)}, bf16[4,256,128]{2,1,0:T(8,1...) while((s32[]{:T(128)}, f32[4,128,128]{2,1,0:T(8,128)S(1)}, ...), condition=%wide.region_2.3_spmd, body=%wide.region_0.2_spmd.sunk | while | flops 27525888 | bytes 128421528 | solution.py:91
  704.5 0.8 constant_dynamic-slice_fusion.2
  705.8 4.5 broadcast_in_dim.19
  710.2 12.9 reshape.129
  723.1 6.4 fusion.25
  729.6 2.5 broadcast_multiply_fusion.4
  732.0 6.1 pad.32
  738.1 17.5 reshape.130
  755.6 4.4 slice_reduce_fusion.2
  760.1 0.6 constant_dynamic-update-slice_fusion.2
  760.8 0.8 constant_dynamic-slice_fusion.2
  761.9 4.5 broadcast_in_dim.19
  766.4 12.9 reshape.129
  779.3 6.4 fusion.25
  785.8 2.5 broadcast_multiply_fusion.4
  788.2 6.1 pad.32
  794.3 17.5 reshape.130
  811.7 4.4 slice_reduce_fusion.2
  816.3 0.6 constant_dynamic-update-slice_fusion.2
  817.0 0.8 constant_dynamic-slice_fusion.2
  818.1 4.5 broadcast_in_dim.19
  822.6 12.9 reshape.129
  835.5 6.4 fusion.25
  841.9 2.5 broadcast_multiply_fusion.4
  844.4 6.1 pad.32
  850.5 17.5 reshape.130
  867.9 4.4 slice_reduce_fusion.2
  872.5 0.6 constant_dynamic-update-slice_fusion.2
  873.2 0.8 constant_dynamic-slice_fusion.2
  874.3 4.5 broadcast_in_dim.19
  878.8 12.9 reshape.129
  891.7 6.4 fusion.25
  898.1 2.5 broadcast_multiply_fusion.4
  900.6 6.1 pad.32
  906.7 17.5 reshape.130
  924.1 4.4 slice_reduce_fusion.2
  928.7 0.6 constant_dynamic-update-slice_fusion.2
  929.4 5.4 convolution_bitcast_fusion
  934.8 9.1 copy.65
  944.0 0.1 rev.23
  944.3 0.8 pad_maximum_fusion
  945.1 540.7 %all-reduce.3.cloned.1.call-done = f32[512,128]{1,0:T(8,128)} async-done(((f32[512,128]{1,0:T(8,128)}), f32[512,128]{1,0:T(8,128)}) %all-reduce.3.cloned.1.call-update) | async-done | bytes 262160 | tf_op jit(solution)/shard_map/psum | solution.py:117
  1485.7 1.7 broadcast_multiply_fusion.1
  1487.4 333.6 %reduce-scatter.4.cloned.1.call-done = f32[64,512]{1,0:T(8,128)} async-done(((f32[4096,512]{1,0:T(8,128)}), f32[64,512]{1,0:T(8,128)}) %reduce-scatter.4.cloned.1.call-update) | async-done | bytes 131088
  1821.0 1.0 copy.66
  1822.1 0.8 copy.52
  (85 shorter events, 3.1 us)
Async XLA Ops:
  7.2 332.2 %all-gather.11.cloned.1.call-start = ((), (), s32[]{:S(2)}) async-start(), calls=%async_computation.4 | async-start | bytes 12779520 | tf_op jit(solution)/shard_map/all_gather | solution.py:45
  7.9 350.9 %all-gather.9.cloned.1.call-start = ((), (), s32[]{:S(2)}) async-start(), calls=%async_computation.3 | async-start | bytes 1310720 | tf_op jit(solution)/shard_map/all_gather | solution.py:42
  8.6 374.7 %all-gather.5.cloned.1.call-start = ((), (), s32[]{:S(2)}) async-start(), calls=%async_computation.1 | async-start | bytes 1310720 | tf_op jit(solution)/shard_map/all_gather | solution.py:43
  9.4 682.4 %all-gather.7.cloned.1.call-start = ((), (), s32[]{:S(2)}) async-start(), calls=%async_computation.2 | async-start | bytes 4259840 | tf_op jit(solution)/shard_map/all_gather | solution.py:52
  10.0 1475.8 %all-reduce.3.cloned.1.call-start = ((), (), s32[]{:S(2)}) async-start(), calls=%async_computation.5 | async-start | bytes 524288 | tf_op jit(solution)/shard_map/psum | solution.py:117
  368.3 336.1 %copy-start.1 = (bf16[128,1,512]{2,0,1:T(8,128)(2,1)}, bf16[128,1,512]{2,0,1:T(8,128)(2,1)S(1)}, u32[]{:S(2)}) copy-start(bf16[128,1,512]{2,0,1:T(8,128)(2,1)S(1)} %copy.74) | copy-start | bytes 393220
  695.7 6.8 collective-permute-start.1
  697.1 7.3 copy-start.2
  697.3 7.2 copy-start.4
  697.3 7.1 collective-permute-start
  704.4 225.0 %copy-start = (bf16[128,4096]{1,0:T(8,128)(2,1)S(1)}, bf16[128,4096]{1,0:T(8,128)(2,1)}, u32[]{:S(2)}) copy-start(bf16[128,4096]{1,0:T(8,128)(2,1)} %all-gather.5.cloned.1.call-done) | copy-start | bytes 3145732
  929.3 891.7 %reduce-scatter.4.cloned.1.call-start = ((), (), s32[]{:S(2)}) async-start(), calls=%async_computation.6 | async-start | bytes 8519680
  934.8 9.3 copy-start.6
  934.8 9.4 copy-start.3
  934.8 9.4 copy-start.5
Sparse Core Ops, SparseCore 0:
  9.8 329.5 all-gather.10
  341.2 17.4 all-gather.8
  360.6 22.7 all-gather.4
  385.0 306.7 all-gather.6
  929.5 556.2 all-reduce.2
  1488.3 332.7 reduce-scatter.3
where the time goes:
time: 1830 us
  waiting for transfers between devices  1530 us (84%)
  local copies, waits for them, and re-layouts  200 us (11%)
  other arithmetic  56.5 us (3%)
  matrix products  18.5 us (1%)
    psum x1, waiting for transfers between devices, on_device(): filter_sum = lax.psum(filter_terms, 'ctx')  541 us
    unnamed x7, waiting for transfers between devices  336 us
    all_gather x1, waiting for transfers between devices, on_device(): piece_rows = lax.all_gather(featurizer, 'ctx', axis=0, tiled=True)  329 us
    all_gather x1, waiting for transfers between devices, on_device(): lax.all_gather(out_weight, 'ctx', axis=0, tiled=True)  308 us
    reshape x4, local copies, waits for them, and re-layouts, one_group(): banded = flat_corr.reshape(group, ntaps, 2 * ntaps + 1)[:, :, 1:ntaps + 1]  69.8 us
    reshape x4, local copies, waits for them, and re-layouts, skew_taps(): tiled.reshape(width_group, ntaps * (2 * ntaps + 1))[:, :2 * ntaps * ntaps]  51.6 us
  transfers between devices with their start and end apart: 8, of which 8 were waited for; matrix products, arithmetic and copies ran while one was open for 2% of the time, Pallas kernels for 0%

commit v1 on v0

v1 whole, which is shorter than its diff:
```python
import functools
import math

import jax
import jax.numpy as jnp
from jax import lax
from jax.experimental import pallas as pl
from jax.experimental.pallas import tpu as pltpu
from jax.sharding import PartitionSpec as P

MESH = pl.DeviceIdType.MESH
BF = jnp.bfloat16
F32 = jnp.float32
NZ = 8
RING = 4


def coords():
    ctx = lax.axis_index("ctx")
    tp = lax.axis_index("tp")
    z = ctx // 8
    y = (ctx // 2) % 4
    xl = ctx % 2
    xh = tp // 2
    core = tp % 2
    return xh, xl, y, z, core


def dev(xh, xl, y, z, core):
    return ((z * 4 + y) * 2 + xl, xh * 2 + core)


def devx(x, y, z, core):
    return dev(x // 2, x % 2, y, z, core)


def slot_of(x):
    return (x % 2) * 2 + x // 2


def remote(src, dst, ssem, rsem, device):
    return pltpu.make_async_remote_copy(
        src_ref=src, dst_ref=dst, send_sem=ssem, recv_sem=rsem, device_id=device, device_id_type=MESH
    )


FP, FM, HP, HM = 0, 1, 2, 3


class Plane:
    def __init__(self, own, buf, ssem, rsem, base, here):
        self.own, self.buf, self.ssem, self.rsem, self.base = own, buf, ssem, rsem, base
        self.x, self.y, self.z, self.core = here
        self.sent = []

    def unit(self, lr, a, b, half):
        dx, dy = (a, b) if lr == 0 else (b, a)
        xx = (self.x + dx) % 4
        yy = (self.y + dy) % 4
        cols = pl.ds(0, 4096) if half is None else pl.ds(half * 2048, 2048)
        return self.buf.at[yy, slot_of(xx), pl.ds(lr * 16, 16), cols]

    def neighbour(self, lr, axis, by):
        if (lr == 0) == (axis == 0):
            return devx((self.x + by) % 4, self.y, self.z, self.core)
        return devx(self.x, (self.y + by) % 4, self.z, self.core)

    def sem(self, lr, axis, a, kind):
        return self.base + lr * 20 + (kind if axis == 0 else 4 + a * 4 + kind)

    def send(self, lr, axis, a, kind):
        by = 1 if kind in (FP, HP) else -1
        back = {FP: 0, FM: 0, HP: 3, HM: 1}[kind]
        half = {FP: None, FM: None, HP: 0, HM: 1}[kind]
        place = (back, 0) if axis == 0 else (a, back)
        dst = self.unit(lr, place[0], place[1], half)
        src = self.own.at[pl.ds(lr * 16, 16), :] if place == (0, 0) else dst
        s = self.sem(lr, axis, a, kind)
        copy = remote(src, dst, self.ssem.at[s], self.rsem.at[s], self.neighbour(lr, axis, by + 4 if by < 0 else by))
        copy.start()
        self.sent.append(copy)

    def wait(self, lr, axis, a, kind):
        off = {FP: 3, FM: 1, HP: 2, HM: 2}[kind]
        half = {FP: None, FM: None, HP: 0, HM: 1}[kind]
        place = (off, 0) if axis == 0 else (a, off)
        dst = self.unit(lr, place[0], place[1], half)
        s = self.sem(lr, axis, a, kind)
        remote(dst, dst, self.ssem.at[s], self.rsem.at[s], self.neighbour(lr, axis, 1)).wait_recv()

    def step1(self):
        for lr in range(2):
            for kind in (FP, FM):
                self.send(lr, 0, 0, kind)
        for lr in range(2):
            for kind in (FP, FM):
                self.send(lr, 1, 0, kind)

    def step2(self):
        for kind, a, hkind in ((FP, 3, HP), (FM, 1, HM)):
            for lr in range(2):
                self.wait(lr, 0, 0, kind)
                self.send(lr, 0, 0, hkind)
                self.send(lr, 1, a, FP)
                self.send(lr, 1, a, FM)

    def step3(self):
        for lr in range(2):
            self.wait(lr, 0, 0, HP)
            self.wait(lr, 0, 0, HM)
            self.send(lr, 1, 2, FP)
            self.send(lr, 1, 2, FM)

    def step4(self, a):
        for kind, hkind in ((FP, HP), (FM, HM)):
            for lr in range(2):
                self.wait(lr, 1, a, kind)
                self.send(lr, 1, a, hkind)

    def step5(self):
        for a in (0, 3, 1, 2):
            for lr in range(2):
                self.wait(lr, 1, a, HP)
                self.wait(lr, 1, a, HM)

    def finish(self):
        for copy in self.sent:
            copy.wait_send()


def gather_kernel(
    x_ref, g_ref, fw_ref, filt_ref,
    qkvg_ref, gext_out, mext_out, taps_out, gall_out,
    xbuf, gbuf, wbuf, acc, gext, mext, filt_recv, filt_own,
    psend, precv, wsend, wrecv, hsend, hrecv, lsem,
):
    xh, xl, y, z, core = coords()
    x = xh * 2 + xl
    here = (x, y, z, core)
    other = 1 - core
    zp, zm = (z + 1) % 8, (z + 7) % 8
    partner = dev(xh, xl, y, z, other)

    barrier = pltpu.get_barrier_semaphore()
    greet = [
        devx((x + 1) % 4, y, z, core), devx((x + 3) % 4, y, z, core),
        devx(x, (y + 1) % 4, z, core), devx(x, (y + 3) % 4, z, core),
        devx(x, y, zp, core), devx(x, y, zm, core),
        devx(x, y, zp, other), devx(x, y, zm, other),
        partner,
        dev(xh, 1 - xl, y, z, other),
    ] + [dev(xh, core, (y + dy) % 4, z, xl) for dy in (1, 2, 3)]
    for d in greet:
        pl.semaphore_signal(barrier, inc=1, device_id=d, device_id_type=MESH)
    pl.semaphore_wait(barrier, len(greet))

    xs = Plane(x_ref, xbuf, psend, precv, 0, here)
    gs = Plane(g_ref, gbuf, psend, precv, 40, here)
    sent = []

    for dy in (1, 2, 3):
        yy = (y + dy) % 4
        c = remote(fw_ref.at[yy], wbuf.at[z, y, xl], wsend.at[dy], wrecv.at[dy], dev(xh, core, yy, z, xl))
        c.start()
        sent.append(c)
    same = xl == core
    own_local = pltpu.make_async_copy(fw_ref.at[y], wbuf.at[z, y, core], lsem.at[0])
    own_remote = remote(
        fw_ref.at[y], wbuf.at[z, y, xl], wsend.at[0], wrecv.at[0], dev(xh, 1 - xl, y, z, other)
    )

    @pl.when(same)
    def _():
        own_local.start()

    @pl.when(jnp.logical_not(same))
    def _():
        own_remote.start()

    filt_copy = remote(filt_ref.at[y], filt_recv, hsend.at[0], hrecv.at[0], partner)
    filt_copy.start()
    sent.append(filt_copy)
    filt_local = pltpu.make_async_copy(filt_ref.at[y], filt_own, lsem.at[1])
    filt_local.start()

    xs.step1()
    x_local = pltpu.make_async_copy(x_ref, xbuf.at[y, slot_of(x)], lsem.at[2])
    x_local.start()
    g_local = pltpu.make_async_copy(g_ref, gbuf.at[y, slot_of(x)], lsem.at[3])
    g_local.start()

    def wblock(zrel, ys=None, e=None):
        e = core if e is None else e
        zz = (z + 8 - zrel) % 8
        return wbuf.at[zz, :, e] if ys is None else wbuf.at[zz, pl.ds(ys, 2), e]

    def wring_send(sem, zrel, ys, to):
        blk = wblock(zrel, ys)
        c = remote(blk, blk, wsend.at[sem], wrecv.at[sem], devx(x, y, to, core))
        c.start()
        sent.append(c)

    def wring_wait(sem, zrel, ys):
        blk = wblock(zrel, ys)
        remote(blk, blk, wsend.at[sem], wrecv.at[sem], devx(x, y, zp, core)).wait_recv()

    def wpair_send(zrel):
        blk = wblock(zrel)
        c = remote(blk, blk, wsend.at[12 + zrel], wrecv.at[12 + zrel], partner)
        c.start()
        sent.append(c)

    def wpair_wait(zrel):
        blk = wblock(zrel, None, other)
        remote(blk, blk, wsend.at[12 + zrel], wrecv.at[12 + zrel], partner).wait_recv()

    @pl.when(same)
    def _():
        own_local.wait()

    @pl.when(jnp.logical_not(same))
    def _():
        own_remote.wait_send()
        remote(
            wbuf.at[z, y, core], wbuf.at[z, y, core], wsend.at[0], wrecv.at[0], dev(xh, 1 - xl, y, z, other)
        ).wait_recv()

    for dy in (1, 2, 3):
        blk = wbuf.at[z, (y + 4 - dy) % 4, core]
        remote(blk, blk, wsend.at[dy], wrecv.at[dy], partner).wait_recv()

    wring_send(4, 0, None, zp)
    wring_send(8, 0, None, zm)
    wpair_send(0)
    xs.step2()
    gs.step1()
    wring_wait(4, 1, None)
    wring_send(5, 1, None, zp)
    wpair_send(1)
    wring_wait(8, 7, None)
    wring_send(9, 7, None, zm)
    wpair_send(7)
    xs.step3()
    xs.step4(0)
    wring_wait(5, 2, None)
    wring_send(6, 2, None, zp)
    wpair_send(2)
    wring_wait(9, 6, None)
    wring_send(10, 6, None, zm)
    wpair_send(6)
    xs.step4(3)
    xs.step4(1)
    gs.step2()
    wring_wait(6, 3, None)
    wring_send(7, 3, 0, zp)
    wpair_send(3)
    wring_wait(10, 5, None)
    wring_send(11, 5, 2, zm)
    wpair_send(5)
    xs.step4(2)
    gs.step3()
    xs.step5()
    wring_wait(7, 4, 0)
    wring_wait(11, 4, 2)
    wpair_send(4)
    gs.step4(0)
    for zrel in range(8):
        wpair_wait(zrel)
    x_local.wait()

    acc[...] = jnp.zeros_like(acc)

    def project_x(i, _):
        cols = pl.ds(pl.multiple_of(i * 512, 512), 512)
        lhs = xbuf[:, :, :, cols].reshape(512, 512)
        rhs = wbuf[i].reshape(512, 512)[:, :384]
        acc[:, 0:384] += jnp.dot(lhs, rhs, preferred_element_type=F32)
        return 0

    lax.fori_loop(0, 8, project_x, 0)

    for i in range(3):
        qkvg_ref[i] = acc[:, i * 128:(i + 1) * 128].astype(BF)
    gated = (qkvg_ref[1].astype(F32) * qkvg_ref[2].astype(F32)).astype(BF)
    gext[pl.ds(2, 16), core] = gated.reshape(16, 32, 128)

    own = gext.at[pl.ds(2, 16), core]
    tail = gext.at[pl.ds(16, 2), core]
    for i, (src, dst, d) in enumerate((
        (own, own, partner),
        (tail, gext.at[pl.ds(0, 2), core], devx(x, y, zp, core)),
        (tail, gext.at[pl.ds(0, 2), core], devx(x, y, zp, other)),
    )):
        c = remote(src, dst, hsend.at[1 + i], hrecv.at[1 + i], d)
        c.start()
        sent.append(c)

    gs.step4(3)
    gs.step4(1)
    gs.step4(2)
    gs.step5()
    g_local.wait()
    gall_copy = pltpu.make_async_copy(gbuf, gall_out, lsem.at[4])
    gall_copy.start()

    def project_g(i, _):
        cols = pl.ds(pl.multiple_of(i * 512, 512), 512)
        lhs = gbuf[:, :, :, cols].reshape(512, 512)
        rhs = wbuf[i].reshape(512, 512)[:, 384:512]
        acc[:, 384:512] += jnp.dot(lhs, rhs, preferred_element_type=F32)
        return 0

    lax.fori_loop(0, 8, project_g, 0)
    qkvg_ref[3] = acc[:, 384:512].astype(BF)
    gmixed = (qkvg_ref[3].astype(F32) * qkvg_ref[0].astype(F32)).astype(BF)
    mext[pl.ds(0, 16), core] = gmixed.reshape(16, 32, 128)
    mown = mext.at[pl.ds(0, 16), core]
    mhead = mext.at[pl.ds(0, 2), core]
    for i, (src, dst, d) in enumerate((
        (mown, mown, partner),
        (mhead, mext.at[pl.ds(16, 2), core], devx(x, y, zm, core)),
        (mhead, mext.at[pl.ds(16, 2), core], devx(x, y, zm, other)),
    )):
        c = remote(src, dst, hsend.at[4 + i], hrecv.at[4 + i], d)
        c.start()
        sent.append(c)

    filt_local.wait()
    filt_copy.wait_recv()
    mine = jnp.where(same, 1.0, 0.0)
    taps_out[...] = filt_own[...].astype(F32) * mine + filt_recv[...].astype(F32) * (1.0 - mine)

    def hwait(i, blk):
        remote(blk, blk, hsend.at[i], hrecv.at[i], partner).wait_recv()

    hwait(1, gext.at[pl.ds(2, 16), other])
    hwait(2, gext.at[pl.ds(0, 2), core])
    hwait(3, gext.at[pl.ds(0, 2), other])
    gext_out[128:1152] = gext[2:18].reshape(1024, 128).astype(F32)
    first = jnp.where(z == 0, 0.0, 1.0)
    gext_out[0:128] = gext[0:2].reshape(128, 128).astype(F32) * first
    hwait(4, mext.at[pl.ds(0, 16), other])
    hwait(5, mext.at[pl.ds(16, 2), core])
    hwait(6, mext.at[pl.ds(16, 2), other])
    mext_out[0:1024] = mext[0:16].reshape(1024, 128).astype(F32)
    last = jnp.where(z == 7, 0.0, 1.0)
    mext_out[1024:1152] = mext[16:18].reshape(128, 128).astype(F32) * last

    gall_copy.wait()
    xs.finish()
    gs.finish()
    for c in sent:
        c.wait_send()


def conv_kernel(qkvg, gext, mext, taps, gall, gf_ref, corr_ref, dwt_ref, corr_acc, mo):
    core = lax.axis_index("tp") % 2
    corr_acc[...] = jnp.zeros_like(corr_acc)

    def chunk(p, _):
        rows = pl.ds(pl.multiple_of(p * 32, 32), 32)
        base = pl.multiple_of((p * 2 + core) * 32, 32)
        q = qkvg[0, rows, :].astype(F32)
        gm = qkvg[3, rows, :].astype(F32)
        m = mext[pl.ds(base, 32), :]

        def taps8(jo, carry):
            mixed, back = carry
            j0 = pl.multiple_of(jo * 8, 8)
            tap = taps[pl.ds(j0, 8), :]
            for ji in range(8):
                f = tap[ji:ji + 1, :]
                g = gext[pl.ds(base + 128 - j0 - ji, 32), :]
                mixed = mixed + f * g
                prod = m * g
                corr_acc[j0 + ji] += (prod[0:8] + prod[8:16]) + (prod[16:24] + prod[24:32])
                back = back + f * mext[pl.ds(base + j0 + ji, 32), :]
            return mixed, back

        zero = jnp.zeros((32, 128), F32)
        mixed, back = lax.fori_loop(0, 16, taps8, (zero, zero))
        mo[rows, :] = (q * mixed).astype(BF)
        gf_ref[p, 0] = (gm * mixed).astype(BF)
        gf_ref[p, 1] = (back * qkvg[2, rows, :].astype(F32)).astype(BF)
        gf_ref[p, 2] = (back * qkvg[1, rows, :].astype(F32)).astype(BF)
        return 0

    lax.fori_loop(0, 16, chunk, 0)
    corr_ref[...] = jnp.sum(corr_acc[...], axis=1)

    mot = mo[...].astype(F32).T.astype(BF)

    def grad_w(i, _):
        for e in range(2):
            cols = pl.ds(pl.multiple_of(i * 512 + e * 256, 256), 256)
            dwt_ref[i, e] = jnp.dot(mot, gall[:, cols], preferred_element_type=F32).astype(BF)
        return 0

    lax.fori_loop(0, 8, grad_w, 0)


def return_kernel(
    scale,
    gf, dwt, corr,
    rgf, dw_out, fout,
    pbuf, sbuf, zbuf, tbuf, dwin, fz, fsum, fpair, ftot, fin,
    gsend, grecv, dsend, drecv, asend, arecv, osend, orecv, fsend, frecv, lsem,
):
    xh, xl, y, z, core = coords()
    x = xh * 2 + xl
    other = 1 - core
    partner = dev(xh, xl, y, z, other)
    same = xl == core
    half = y // 2

    barrier = pltpu.get_barrier_semaphore()
    pl.semaphore_signal(barrier, inc=1, device_id=partner, device_id_type=MESH)
    for r in range(1, 8):
        pl.semaphore_signal(barrier, inc=1, device_id=devx(x, y, (z + r) % 8, core), device_id_type=MESH)
    for ys in range(4):
        for cs in range(2):
            me = jnp.logical_and(same, jnp.logical_and(y == ys, core == cs))

            @pl.when(jnp.logical_not(me))
            def _():
                pl.semaphore_signal(barrier, inc=1, device_id=dev(xh, core, ys, z, cs), device_id_type=MESH)

    pl.semaphore_wait(barrier, 16 - jnp.where(same, 1, 0))

    order = (4, 3, 5, 2, 6, 1, 7, 0)
    for r in order:
        zz = (z + r) % 8
        remote(dwt.at[zz, other], pbuf.at[r], dsend.at[r], drecv.at[r], partner).start()
    for r in range(1, 8):
        zz = (z + r) % 8
        remote(corr.at[zz], fz.at[r], fsend.at[r], frecv.at[r], devx(x, y, zz, core)).start()

    def gf_copy(yp, xp):
        return remote(
            gf.at[pl.ds((yp * 2 + xp) * 2, 2)], rgf.at[y, core], gsend.at[yp * 2 + xp],
            grecv.at[y * 2 + core], dev(xh, xp, yp, z, xl),
        )

    def gf_self(yp, xp):
        return jnp.logical_and(same, jnp.logical_and(y == yp, xl == xp))

    gf_local = pltpu.make_async_copy(gf.at[pl.ds((y * 2 + xl) * 2, 2)], rgf.at[y, core], lsem.at[0])

    @pl.when(same)
    def _():
        gf_local.start()

    for yp in range(4):
        for xp in range(2):
            @pl.when(jnp.logical_not(gf_self(yp, xp)))
            def _():
                gf_copy(yp, xp).start()

    for r in order:
        zz = (z + r) % 8
        remote(pbuf.at[r], pbuf.at[r], dsend.at[r], drecv.at[r], partner).wait_recv()
        both = dwt[zz, core].astype(F32) + pbuf[r].astype(F32)
        sbuf[r] = both.astype(BF)
        if r:
            remote(sbuf.at[r], zbuf.at[r], asend.at[r], arecv.at[r], devx(x, y, zz, core)).start()

    fs = corr[z]
    for r in range(1, 8):
        remote(fz.at[r], fz.at[r], fsend.at[r], frecv.at[r], partner).wait_recv()
        fs = fs + fz[r]
    fsum[...] = fs
    fpair_copy = remote(fsum, fpair, fsend.at[0], frecv.at[0], partner)
    fpair_copy.start()
    fpair_copy.wait_recv()
    ftot[...] = (fsum[...] + fpair[...]) * scale

    fin_local = pltpu.make_async_copy(ftot, fin.at[y], lsem.at[1])

    def f_copy(yp):
        return remote(ftot, fin.at[y], fsend.at[8 + yp], frecv.at[8 + y], dev(xh, core, yp, z, xl))

    def f_self(yp):
        return jnp.logical_and(same, y == yp)

    @pl.when(same)
    def _():
        fin_local.start()

    for yp in range(4):
        @pl.when(jnp.logical_not(f_self(yp)))
        def _():
            f_copy(yp).start()

    total = sbuf[0].astype(F32)
    for r in (1, 7, 2, 6, 3, 5, 4):
        remote(zbuf.at[r], zbuf.at[r], asend.at[r], arecv.at[r], partner).wait_recv()
        total = total + zbuf[r].astype(F32)
    tbuf[...] = (total.T * scale).reshape(4, 64, 128)

    def dw_copy(k):
        yp, xp = core * 2 + k // 2, k % 2
        return remote(tbuf.at[k], dwin.at[y], osend.at[k], orecv.at[y], dev(xh, xp, yp, z, xl))

    def dw_self(k):
        yp, xp = core * 2 + k // 2, k % 2
        return jnp.logical_and(same, jnp.logical_and(y == yp, xl == xp))

    dw_here = jnp.logical_and(same, half == core)
    dw_local = pltpu.make_async_copy(tbuf.at[(y % 2) * 2 + xl], dwin.at[y], lsem.at[2])

    @pl.when(dw_here)
    def _():
        dw_local.start()

    for k in range(4):
        @pl.when(jnp.logical_not(dw_self(k)))
        def _():
            dw_copy(k).start()

    @pl.when(same)
    def _():
        fin_local.wait()

    for ys in range(4):
        @pl.when(jnp.logical_not(f_self(ys)))
        def _():
            remote(fin.at[ys], fin.at[ys], fsend.at[8 + ys], frecv.at[8 + ys], partner).wait_recv()
    for r in range(1, 8):
        remote(fin, fout.at[z], fsend.at[12 + r], frecv.at[12 + r], devx(x, y, (z + r) % 8, core)).start()
    fout_local = pltpu.make_async_copy(fin, fout.at[z], lsem.at[3])
    fout_local.start()

    @pl.when(dw_here)
    def _():
        dw_local.wait()

    for ys in range(4):
        @pl.when(jnp.logical_not(jnp.logical_and(dw_here, y == ys)))
        def _():
            remote(dwin.at[ys], dwin.at[ys], osend.at[ys], orecv.at[ys], partner).wait_recv()
        dw_out[:, ys * 128:(ys + 1) * 128] = dwin[ys]

    @pl.when(same)
    def _():
        gf_local.wait()

    for ys in range(4):
        for cs in range(2):
            me = jnp.logical_and(same, jnp.logical_and(y == ys, core == cs))

            @pl.when(jnp.logical_not(me))
            def _():
                blk = rgf.at[ys, cs]
                remote(blk, blk, gsend.at[0], grecv.at[ys * 2 + cs], partner).wait_recv()
    fout_local.wait()
    for r in range(1, 8):
        blk = fout.at[(z + 8 - r) % 8]
        remote(blk, blk, fsend.at[12 + r], frecv.at[12 + r], partner).wait_recv()

    for r in order:
        zz = (z + r) % 8
        remote(dwt.at[zz, other], pbuf.at[r], dsend.at[r], drecv.at[r], partner).wait_send()
        if r:
            remote(sbuf.at[r], zbuf.at[r], asend.at[r], arecv.at[r], partner).wait_send()
            remote(corr.at[zz], fz.at[r], fsend.at[r], frecv.at[r], partner).wait_send()
            remote(fin, fout.at[z], fsend.at[12 + r], frecv.at[12 + r], partner).wait_send()
    fpair_copy.wait_send()
    for yp in range(4):
        for xp in range(2):
            @pl.when(jnp.logical_not(gf_self(yp, xp)))
            def _():
                gf_copy(yp, xp).wait_send()

        @pl.when(jnp.logical_not(f_self(yp)))
        def _():
            f_copy(yp).wait_send()

        @pl.when(jnp.logical_not(dw_self(yp)))
        def _():
            dw_copy(yp).wait_send()


VM = pl.BlockSpec(memory_space=pltpu.VMEM)
ANY = pl.BlockSpec(memory_space=pl.ANY)
DMA = pltpu.SemaphoreType.DMA


def sds(shape, dtype):
    return jax.ShapeDtypeStruct(shape, dtype)


def on_device(block_input, featurizer, filters, out_weight, grad_output):
    f4 = featurizer.reshape(64, 3, 4, 128)
    w4 = out_weight.reshape(64, 1, 4, 128)
    fw = jnp.concatenate([f4, w4], axis=1).transpose(2, 0, 1, 3).reshape(4, 64, 512)
    filt = filters.reshape(4, 128, 128).transpose(0, 2, 1)

    qkvg, gext, mext, taps, gall = pl.pallas_call(
        gather_kernel,
        out_shape=(
            sds((4, 512, 128), BF), sds((1152, 128), F32), sds((1152, 128), F32), sds((128, 128), F32),
            sds((4, 4, 32, 4096), BF),
        ),
        in_specs=[ANY] * 4,
        out_specs=(VM, VM, VM, VM, ANY),
        scratch_shapes=[
            pltpu.VMEM((4, 4, 32, 4096), BF),
            pltpu.VMEM((4, 4, 32, 4096), BF),
            pltpu.VMEM((8, 4, 2, 64, 512), BF),
            pltpu.VMEM((512, 512), F32),
            pltpu.VMEM((18, 2, 32, 128), BF),
            pltpu.VMEM((18, 2, 32, 128), BF),
            pltpu.VMEM((128, 128), BF),
            pltpu.VMEM((128, 128), BF),
            DMA((80,)), DMA((80,)), DMA((20,)), DMA((20,)), DMA((7,)), DMA((7,)), DMA((5,)),
        ],
        compiler_params=pltpu.CompilerParams(
            collective_id=1, has_side_effects=True, vmem_limit_bytes=40 * 2**20
        ),
        name="gather_project",
    )(block_input, grad_output, fw, filt)

    gf, corr, dwt = pl.pallas_call(
        conv_kernel,
        out_shape=(sds((16, 3, 32, 128), BF), sds((128, 128), F32), sds((8, 2, 128, 256), BF)),
        in_specs=[VM] * 5,
        out_specs=(VM, VM, VM),
        scratch_shapes=[pltpu.VMEM((128, 8, 128), F32), pltpu.VMEM((512, 128), BF)],
        compiler_params=pltpu.CompilerParams(vmem_limit_bytes=40 * 2**20),
        name="filter_local",
    )(qkvg, gext, mext, taps, gall.reshape(512, 4096))

    scale = 1.0 / math.sqrt(128 * lax.axis_size("ctx"))
    rgf, dw, fout = pl.pallas_call(
        functools.partial(return_kernel, scale),
        out_shape=(sds((4, 2, 2, 3, 32, 128), BF), sds((64, 512), F32), sds((8, 4, 16, 128), F32)),
        in_specs=[VM] * 3,
        out_specs=(VM, VM, VM),
        scratch_shapes=[
            pltpu.VMEM((8, 128, 256), BF),
            pltpu.VMEM((8, 128, 256), BF),
            pltpu.VMEM((8, 128, 256), BF),
            pltpu.VMEM((4, 64, 128), F32),
            pltpu.VMEM((4, 64, 128), F32),
            pltpu.VMEM((8, 16, 128), F32),
            pltpu.VMEM((16, 128), F32),
            pltpu.VMEM((16, 128), F32),
            pltpu.VMEM((16, 128), F32),
            pltpu.VMEM((4, 16, 128), F32),
            DMA((8,)), DMA((8,)), DMA((8,)), DMA((8,)), DMA((8,)), DMA((8,)), DMA((4,)), DMA((4,)),
            DMA((20,)), DMA((20,)), DMA((4,)),
        ],
        compiler_params=pltpu.CompilerParams(
            collective_id=2, has_side_effects=True, vmem_limit_bytes=40 * 2**20
        ),
        name="sum_return",
    )(gf, dwt, corr.reshape(8, 16, 128))

    grad_features = rgf.transpose(2, 1, 4, 3, 0, 5).reshape(128, 3, 512)
    grad_filters = fout.transpose(1, 3, 0, 2).reshape(512, 128)
    return grad_features, dw, grad_filters


def solution(mesh):
    placed = (
        P(("ctx", "tp"), None),
        P("ctx", None, "tp"),
        P("tp", None),
        P("ctx", "tp"),
        P(("ctx", "tp"), None),
    )
    return jax.shard_map(
        on_device,
        mesh=mesh,
        in_specs=placed,
        out_specs=(P("ctx", None, "tp"), P("ctx", "tp"), P("tp", None)),
        check_vma=False,
    )
```

time: 1830 us -> 116 us (0.06)
  waiting for transfers between devices: 1530 us -> 0 us
  local copies, waits for them, and re-layouts: 200 us -> 7.96 us
  Pallas kernels: 0 us -> 105 us
  other arithmetic: 56.5 us -> 0.28 us
  matrix products: 18.5 us -> 0 us
    all_gather x4 -> x0, waiting for transfers between devices: 655 us -> none  [the longest x1 329 us: on_device(): piece_rows = lax.all_gather(featurizer, 'ctx', axis=0, tiled=True)]
    psum x1 -> x0, waiting for transfers between devices: 541 us -> none  [on_device(): filter_sum = lax.psum(filter_terms, 'ctx')]
    unnamed x7 -> x0, waiting for transfers between devices: 336 us -> none
    reshape x9 -> x7, local copies, waits for them, and re-layouts: 121 us -> 4.14 us  [the longest x2 1.15 us: on_device(): f4 = featurizer.reshape(64, 3, 4, 128)]
    pallas_call x0 -> x3, Pallas kernels: none -> 105 us  [the longest x1 64.2 us: on_device(): pl.pallas_call(gather_kernel, out_shape=(sds((4, 512, 128), BF), sds((115...]
    dot_general x8 -> x0, other arithmetic: 35.3 us -> none  [the longest x4 25.5 us: one_group(): jnp.einsum('ciw,bwc->bic', toeplitz, reversed_windows, preferred_element_...]
    pad x4 -> x0, local copies, waits for them, and re-layouts: 24.3 us -> none  [one_group(): jnp.pad(correl.reshape(group, 2 * ntaps * ntaps), ((0, 0), (0, ntaps)))]
    dot_general x3 -> x0, matrix products: 18.5 us -> none  [the longest x1 9.19 us: on_device(): projected = jnp.dot(columns, flat_piece, preferred_element_type=jnp.float32)]
  transfers between devices with their start and end apart: 8 -> 0, of which waited for: 8 -> 0; matrix products, arithmetic and copies ran while one was open for 2% -> 0% of each run, Pallas kernels for 0% -> 0%
where the time goes in v1:
time: 116 us; the launch traced here: 114 us
  Pallas kernels  105 us (91%)
  local copies, waits for them, and re-layouts  7.96 us (7%)
    pallas_call x1, Pallas kernels, on_device(): pl.pallas_call(gather_kernel, out_shape=(sds((4, 512, 128), BF), sds((115...  64.2 us
    pallas_call x1, Pallas kernels, on_device(): pl.pallas_call(functools.partial(return_kernel, scale), out_shape=(sds((4...  30.3 us
    pallas_call x1, Pallas kernels, on_device(): pl.pallas_call(conv_kernel, out_shape=(sds((16, 3, 32, 128), BF), sds((12...  10.9 us
    unnamed x7, local copies, waits for them, and re-layouts  3.41 us

profile of v1, /device:TPU:4, one launch (start us, length us, event | category | flops | bytes accessed | tf_op | source)
XLA Modules:
  0.0 114.4 jit_solution(13635757635746548166)
XLA Ops:
  0.6 0.9 reshape.31
  1.5 0.1 copy.11
  1.6 1.0 copy.12
  2.6 1.0 reshape.30
  3.6 0.2 copy.10
  3.8 0.3 maximum_bitcast_fusion
  4.1 0.1 reshape.32.fw_ref
  4.2 0.0 copy-start
  4.2 0.9 copy-done
  5.1 0.0 copy-start.1
  5.1 0.9 copy-done.1
  6.1 64.2 %gather_project.1 = (bf16[4,512,128]{2,1,0:T(8,128)(2,1)S(1)}, f32[1152,128]{1,0:T(8,128)S(1)}, f32[1152,128]{1,0:T(8,128)S(1)}, f32[128,128]{1,0:T(8,128)S(1)}, bf16[4,4,32,4096]{3,2,1,0:T(8,128)(2,1)S(1)}) custom-call(bf16[32,4096]{1,0:T(8,128)(2,1)S(1)} %copy-done, bf16[32,4096]{1,0:T(8,128)(2,1)S(1)} %copy-done.1, ...), custom_call_target="tpu_custom_call" | custom-call | tf_op jit(solution)/shard_map/gather_project/pallas_call | solution.py:598
  70.3 10.9 %filter_local.1 = (bf16[16,3,32,128]{3,2,1,0:T(8,128)(2,1)S(1)}, f32[128,128]{1,0:T(8,128)S(1)}, bf16[8,2,128,256]{3,2,1,0:T(8,128)(2,1)S(1)}) custom-call(bf16[4,512,128]{2,1,0:T(8,128)(2,1)S(1)} %get-tuple-element.14.qkvg, f32[1152,128]{1,0:T(8,128)S(1)} %get-tuple-element.15.gext, f32[1152,128]{1,0:T(8,128)S(1)} %get-tuple-element.16.mext, ...), custom_call_target="tpu_custom_call" | custom-call | tf_op jit(solution)/shard_map/filter_local/pallas_call | solution.py:623
  81.3 30.3 %sum_return.1 = (bf16[4,2,2,3,32,128]{5,4,3,2,1,0:T(8,128)(2,1)S(1)}, f32[64,512]{1,0:T(8,128)S(1)}, f32[8,4,16,128]{3,2,1,0:T(8,128)S(1)}) custom-call(bf16[16,3,32,128]{3,2,1,0:T(8,128)(2,1)S(1)} %get-tuple-element.19.gf, bf16[8,2,128,256]{3,2,1,0:T(8,128)(2,1)S(1)} %get-tuple-element.20.dwt, f32[8,16,128]{2,1,0:T(8,128)S(1)} %bitcast.23), custom_call_target="tpu_custom_call" | custom-call | tf_op jit(solution)/shard_map/sum_return/pallas_call | solution.py:634
  111.6 0.3 copy.13
  111.9 0.9 reshape.36
  112.8 0.1 copy.14
  112.9 0.8 copy.15
  113.8 0.7 copy.20
  (1 shorter events, 0.0 us)
Async XLA Ops:
  4.2 1.0 copy-start
  5.1 0.9 copy-start.1

commit v2 on v1

v2 whole, which is shorter than its diff:
```python
import functools
import math

import jax
import jax.numpy as jnp
from jax import lax
from jax.experimental import pallas as pl
from jax.experimental.pallas import tpu as pltpu
from jax.sharding import PartitionSpec as P

MESH = pl.DeviceIdType.MESH
BF = jnp.bfloat16
F32 = jnp.float32
FP, FM, HP, HM = 0, 1, 2, 3
FAR = ((4, 3, 5, 2), (6, 1, 7, 0))


def coords():
    ctx = lax.axis_index("ctx")
    tp = lax.axis_index("tp")
    z = ctx // 8
    y = (ctx // 2) % 4
    xl = ctx % 2
    xh = tp // 2
    core = tp % 2
    return xh, xl, y, z, core


def dev(xh, xl, y, z, core):
    return ((z * 4 + y) * 2 + xl, xh * 2 + core)


def devx(x, y, z, core):
    return dev(x // 2, x % 2, y, z, core)


def slot_of(x):
    return (x % 2) * 2 + x // 2


def remote(src, dst, ssem, rsem, device):
    return pltpu.make_async_remote_copy(
        src_ref=src, dst_ref=dst, send_sem=ssem, recv_sem=rsem, device_id=device, device_id_type=MESH
    )


class Plane:
    def __init__(self, place, ssem, rsem, base, here):
        self.place, self.ssem, self.rsem, self.base = place, ssem, rsem, base
        self.x, self.y, self.z, self.core = here
        self.sent = []

    def unit(self, lr, a, b, half):
        dx, dy = (a, b) if lr == 0 else (b, a)
        return self.place((self.y + dy) % 4, slot_of((self.x + dx) % 4), lr, half)

    def neighbour(self, lr, axis, by):
        if (lr == 0) == (axis == 0):
            return devx((self.x + by) % 4, self.y, self.z, self.core)
        return devx(self.x, (self.y + by) % 4, self.z, self.core)

    def sem(self, lr, axis, a, kind):
        return self.base + lr * 20 + (kind if axis == 0 else 4 + a * 4 + kind)

    def send(self, lr, axis, a, kind):
        by = 1 if kind in (FP, HP) else 3
        back = {FP: 0, FM: 0, HP: 3, HM: 1}[kind]
        half = {FP: None, FM: None, HP: 0, HM: 1}[kind]
        place = (back, 0) if axis == 0 else (a, back)
        ref = self.unit(lr, place[0], place[1], half)
        s = self.sem(lr, axis, a, kind)
        copy = remote(ref, ref, self.ssem.at[s], self.rsem.at[s], self.neighbour(lr, axis, by))
        copy.start()
        self.sent.append(copy)

    def wait(self, lr, axis, a, kind):
        off = {FP: 3, FM: 1, HP: 2, HM: 2}[kind]
        half = {FP: None, FM: None, HP: 0, HM: 1}[kind]
        place = (off, 0) if axis == 0 else (a, off)
        dst = self.unit(lr, place[0], place[1], half)
        s = self.sem(lr, axis, a, kind)
        remote(dst, dst, self.ssem.at[s], self.rsem.at[s], self.neighbour(lr, axis, 1)).wait_recv()

    def step1(self):
        for axis in range(2):
            for lr in range(2):
                for kind in (FP, FM):
                    self.send(lr, axis, 0, kind)

    def step2(self):
        for kind, a, hkind in ((FP, 3, HP), (FM, 1, HM)):
            for lr in range(2):
                self.wait(lr, 0, 0, kind)
                self.send(lr, 0, 0, hkind)
                self.send(lr, 1, a, FP)
                self.send(lr, 1, a, FM)

    def step3(self):
        for lr in range(2):
            self.wait(lr, 0, 0, HP)
            self.wait(lr, 0, 0, HM)
            self.send(lr, 1, 2, FP)
            self.send(lr, 1, 2, FM)

    def step4(self, a):
        for kind, hkind in ((FP, HP), (FM, HM)):
            for lr in range(2):
                self.wait(lr, 1, a, kind)
                self.send(lr, 1, a, hkind)

    def step5(self):
        for a in (0, 3, 1, 2):
            for lr in range(2):
                self.wait(lr, 1, a, HP)
                self.wait(lr, 1, a, HM)

    def finish(self):
        for copy in self.sent:
            copy.wait_send()


def block_kernel(
    scale,
    x_ref, g_ref, f_ref, w_ref, filt_ref,
    gfo, dw_out, fo,
    xbuf, gbuf, wbuf, wst, fst, filt_recv, acc, qkvg, gext, mext, gx, mx, taps, corr_acc, corr, mo,
    gfb, dsend_buf, down, pbuf, sbuf, zbuf, tbuf, fz, ftot, fin, fout,
    psend, precv, wsend, wrecv, hsend, hrecv, gsend, grecv, dsend, drecv, asend, arecv, osend, orecv, fsend, frecv,
    lsem,
):
    xh, xl, y, z, core = coords()
    x = xh * 2 + xl
    here = (x, y, z, core)
    other = 1 - core
    zp, zm = (z + 1) % 8, (z + 7) % 8
    partner = dev(xh, xl, y, z, other)
    same = xl == core
    apart = jnp.logical_not(same)
    me_slot = slot_of(x)

    barrier = pltpu.get_barrier_semaphore()
    greet = [
        devx((x + 1) % 4, y, z, core), devx((x + 3) % 4, y, z, core),
        devx(x, (y + 1) % 4, z, core), devx(x, (y + 3) % 4, z, core),
        partner,
        dev(xh, 1 - xl, y, z, other),
    ] + [dev(xh, core, (y + dy) % 4, z, xl) for dy in (1, 2, 3)]
    for r in range(1, 8):
        greet += [devx(x, y, (z + r) % 8, core), devx(x, y, (z + r) % 8, other)]
    for d in greet:
        pl.semaphore_signal(barrier, inc=1, device_id=d, device_id_type=MESH)
    for ys in range(4):
        for cs in range(2):
            me = jnp.logical_and(same, jnp.logical_and(y == ys, core == cs))

            @pl.when(jnp.logical_not(me))
            def _():
                pl.semaphore_signal(barrier, inc=1, device_id=dev(xh, core, ys, z, cs), device_id_type=MESH)

    stage = [
        pltpu.make_async_copy(f_ref, wst.at[pl.ds(0, 3)], lsem.at[0]),
        pltpu.make_async_copy(w_ref, wst.at[3], lsem.at[1]),
        pltpu.make_async_copy(x_ref, xbuf.at[y, me_slot], lsem.at[2]),
        pltpu.make_async_copy(filt_ref.at[pl.ds(pl.multiple_of(y * 128, 128), 128)], fst, lsem.at[3]),
    ]
    for h in range(2):
        for k in range(4):
            zz = (z + FAR[h][k]) % 8
            stage.append(pltpu.make_async_copy(
                g_ref.at[:, pl.ds(pl.multiple_of(zz * 512, 512), 512)], gbuf.at[h, y, me_slot, k], lsem.at[4 + h * 4 + k]
            ))
    for c in stage:
        c.start()
    for c in stage:
        c.wait()
    pl.semaphore_wait(barrier, len(greet) + 8 - jnp.where(same, 1, 0))

    def place_x(yy, s, lr, half):
        cols = pl.ds(0, 4096) if half is None else pl.ds(half * 2048, 2048)
        return xbuf.at[yy, s, pl.ds(lr * 16, 16), cols]

    def place_g(h):
        def place(yy, s, lr, half):
            ks = pl.ds(0, 4) if half is None else pl.ds(half * 2, 2)
            return gbuf.at[h, yy, s, ks, pl.ds(lr * 16, 16), :]
        return place

    xs = Plane(place_x, psend, precv, 0, here)
    ga = Plane(place_g(0), psend, precv, 40, here)
    gb = Plane(place_g(1), psend, precv, 80, here)
    sent = []

    def start(c):
        c.start()
        sent.append(c)

    def wslice(yy):
        return wst.at[:, :, pl.ds(pl.multiple_of(yy * 128, 128), 128)]

    for dy in (1, 2, 3):
        yy = (y + dy) % 4
        start(remote(wslice(yy), wbuf.at[z, :, y, xl], wsend.at[dy], wrecv.at[dy], dev(xh, core, yy, z, xl)))
    own_local = pltpu.make_async_copy(wslice(y), wbuf.at[z, :, y, core], lsem.at[12])
    own_remote = remote(
        wslice(y), wbuf.at[z, :, y, xl], wsend.at[0], wrecv.at[0], dev(xh, 1 - xl, y, z, other)
    )

    @pl.when(same)
    def _():
        own_local.start()

    @pl.when(apart)
    def _():
        own_remote.start()

    filt_copy = remote(fst, filt_recv, hsend.at[0], hrecv.at[0], partner)
    start(filt_copy)
    xs.step1()

    def wblock(zrel, kinds=None, e=None):
        e = core if e is None else e
        zz = (z + 8 - zrel) % 8
        return wbuf.at[zz, :, :, e] if kinds is None else wbuf.at[zz, pl.ds(kinds, 2), :, e]

    def wring_send(sem, zrel, kinds, to):
        blk = wblock(zrel, kinds)
        start(remote(blk, blk, wsend.at[sem], wrecv.at[sem], devx(x, y, to, core)))

    def wring_wait(sem, zrel, kinds):
        blk = wblock(zrel, kinds)
        remote(blk, blk, wsend.at[sem], wrecv.at[sem], devx(x, y, zp, core)).wait_recv()

    def wpair_send(zrel):
        blk = wblock(zrel)
        start(remote(blk, blk, wsend.at[12 + zrel], wrecv.at[12 + zrel], partner))

    def wpair_wait(zrel):
        blk = wblock(zrel, None, other)
        remote(blk, blk, wsend.at[12 + zrel], wrecv.at[12 + zrel], partner).wait_recv()

    @pl.when(same)
    def _():
        own_local.wait()

    @pl.when(apart)
    def _():
        blk = wbuf.at[z, :, y, core]
        own_remote.wait_send()
        remote(blk, blk, wsend.at[0], wrecv.at[0], dev(xh, 1 - xl, y, z, other)).wait_recv()

    for dy in (1, 2, 3):
        blk = wbuf.at[z, :, (y + 4 - dy) % 4, core]
        remote(blk, blk, wsend.at[dy], wrecv.at[dy], partner).wait_recv()

    wring_send(4, 0, None, zp)
    wring_send(8, 0, None, zm)
    wpair_send(0)
    xs.step2()
    wring_wait(4, 1, None)
    wring_send(5, 1, None, zp)
    wpair_send(1)
    wring_wait(8, 7, None)
    wring_send(9, 7, None, zm)
    wpair_send(7)
    xs.step3()
    xs.step4(0)
    wring_wait(5, 2, None)
    wring_send(6, 2, None, zp)
    wpair_send(2)
    wring_wait(9, 6, None)
    wring_send(10, 6, None, zm)
    wpair_send(6)
    ga.step1()
    xs.step4(3)
    xs.step4(1)
    wring_wait(6, 3, None)
    wring_send(7, 3, 0, zp)
    wpair_send(3)
    wring_wait(10, 5, None)
    wring_send(11, 5, 2, zm)
    wpair_send(5)
    xs.step4(2)
    ga.step2()
    xs.step5()
    wring_wait(7, 4, 0)
    wring_wait(11, 4, 2)
    wpair_send(4)
    ga.step3()
    ga.step4(0)
    for zrel in range(8):
        wpair_wait(zrel)

    acc[...] = jnp.zeros_like(acc)

    def project_x(i, _):
        cols = pl.ds(pl.multiple_of(i * 512, 512), 512)
        lhs = xbuf[:, :, :, cols].reshape(512, 512)
        rhs = jnp.concatenate([wbuf[i, kind].reshape(512, 128) for kind in range(3)], axis=1)
        acc[:, 0:384] += jnp.dot(lhs, rhs, preferred_element_type=F32)
        return 0

    lax.fori_loop(0, 4, project_x, 0)
    ga.step4(3)
    gb.step1()
    lax.fori_loop(4, 8, project_x, 0)
    ga.step4(1)

    for i in range(3):
        qkvg[i] = acc[:, i * 128:(i + 1) * 128].astype(BF)
    gated = (qkvg[1].astype(F32) * qkvg[2].astype(F32)).astype(BF)
    gext[pl.ds(2, 16), core] = gated.reshape(16, 32, 128)

    own = gext.at[pl.ds(2, 16), core]
    tail = gext.at[pl.ds(16, 2), core]
    head = gext.at[pl.ds(0, 2), core]
    start(remote(own, own, hsend.at[1], hrecv.at[1], partner))
    start(remote(tail, head, hsend.at[2], hrecv.at[2], devx(x, y, zp, core)))
    start(remote(tail, head, hsend.at[3], hrecv.at[3], devx(x, y, zp, other)))
    ga.step4(2)
    gb.step2()
    ga.step5()

    def project_g(h, k):
        lhs = gbuf[h, :, :, k].reshape(512, 512)
        rhs = wbuf[(z + FAR[h][k]) % 8, 3].reshape(512, 128)
        return jnp.dot(lhs, rhs, preferred_element_type=F32)

    acc[:, 384:512] = project_g(0, 0) + project_g(0, 1)
    gb.step3()
    acc[:, 384:512] += project_g(0, 2) + project_g(0, 3)

    filt_copy.wait_recv()
    mine = jnp.where(same, 1.0, 0.0)
    taps[...] = (fst[...].astype(F32) * mine + filt_recv[...].astype(F32) * (1.0 - mine)).T

    def hwait(i, blk):
        remote(blk, blk, hsend.at[i], hrecv.at[i], partner).wait_recv()

    hwait(1, gext.at[pl.ds(2, 16), other])
    hwait(2, gext.at[pl.ds(0, 2), core])
    hwait(3, gext.at[pl.ds(0, 2), other])
    first = jnp.where(z == 0, 0.0, 1.0)
    gx[0:128] = gext[0:2].reshape(128, 128).astype(F32) * first
    gx[128:1152] = gext[2:18].reshape(1024, 128).astype(F32)
    gb.step4(0)

    zero = jnp.zeros((32, 128), F32)

    def rows_of(i):
        lo = pl.multiple_of(i * 64, 64)
        return pl.ds(lo, 32), pl.ds(lo + 32, 32), pl.multiple_of((i * 4 + core) * 32, 32)

    def mixed_pair(i, _):
        r0, r1, base = rows_of(i)

        def taps8(jo, carry):
            m0, m1 = carry
            j0 = pl.multiple_of(jo * 8, 8)
            tap = taps[pl.ds(j0, 8), :]
            for ji in range(8):
                f = tap[ji:ji + 1, :]
                m0 = m0 + f * gx[pl.ds(base + 128 - j0 - ji, 32), :]
                m1 = m1 + f * gx[pl.ds(base + 192 - j0 - ji, 32), :]
            return m0, m1

        m0, m1 = lax.fori_loop(0, 16, taps8, (zero, zero))
        acc[r0, 0:128] = m0
        acc[r1, 0:128] = m1
        return 0

    lax.fori_loop(0, 3, mixed_pair, 0)
    gb.step4(3)
    lax.fori_loop(3, 6, mixed_pair, 0)
    gb.step4(1)
    lax.fori_loop(6, 8, mixed_pair, 0)
    mo[...] = (qkvg[0].astype(F32) * acc[:, 0:128]).T.astype(BF)
    gb.step4(2)

    def grad_w(h, k):
        def term(e):
            cols = pl.ds(pl.multiple_of(e * 256, 256), 256)
            rhs = gbuf[h, :, :, k, :, cols].reshape(512, 256)
            return jnp.dot(mo[...], rhs, preferred_element_type=F32)

        i = h * 4 + k
        dsend_buf[i] = term(other).astype(BF)
        start(remote(dsend_buf.at[i], pbuf.at[i], dsend.at[i], drecv.at[i], partner))
        down[i] = term(core)

    def both_cores(h, k):
        i, r = h * 4 + k, FAR[h][k]
        remote(pbuf.at[i], pbuf.at[i], dsend.at[i], drecv.at[i], partner).wait_recv()
        down[i] = down[i] + pbuf[i].astype(F32)
        if r:
            sbuf[i] = down[i].astype(BF)
            start(remote(sbuf.at[i], zbuf.at[i], asend.at[i], arecv.at[i], devx(x, y, (z + r) % 8, core)))

    for k in range(4):
        grad_w(0, k)
    gb.step5()
    acc[:, 384:512] += project_g(1, 0) + project_g(1, 1)
    for k in range(4):
        both_cores(0, k)
    acc[:, 384:512] += project_g(1, 2) + project_g(1, 3)

    qkvg[3] = acc[:, 384:512].astype(BF)
    gmixed = (qkvg[3].astype(F32) * qkvg[0].astype(F32)).astype(BF)
    mext[pl.ds(0, 16), core] = gmixed.reshape(16, 32, 128)
    mown = mext.at[pl.ds(0, 16), core]
    mhead = mext.at[pl.ds(0, 2), core]
    mtail = mext.at[pl.ds(16, 2), core]
    start(remote(mown, mown, hsend.at[4], hrecv.at[4], partner))
    start(remote(mhead, mtail, hsend.at[5], hrecv.at[5], devx(x, y, zm, core)))
    start(remote(mhead, mtail, hsend.at[6], hrecv.at[6], devx(x, y, zm, other)))
    for k in range(4):
        grad_w(1, k)

    corr_acc[...] = jnp.zeros_like(corr_acc)

    def corr_pair(i, _):
        _, _, base = rows_of(i)
        c0 = mext[pl.ds(i * 2, 1), core].reshape(32, 128).astype(F32)
        c1 = mext[pl.ds(i * 2 + 1, 1), core].reshape(32, 128).astype(F32)

        def taps8(jo, _):
            j0 = pl.multiple_of(jo * 8, 8)
            for ji in range(8):
                p = c0 * gx[pl.ds(base + 128 - j0 - ji, 32), :] + c1 * gx[pl.ds(base + 192 - j0 - ji, 32), :]
                corr_acc[j0 + ji] += (p[0:8] + p[8:16]) + (p[16:24] + p[24:32])
            return 0

        lax.fori_loop(0, 16, taps8, 0)
        return 0

    lax.fori_loop(0, 8, corr_pair, 0)
    corr[...] = jnp.sum(corr_acc[...], axis=1).reshape(8, 2, 8, 128)
    for r in range(8):
        zz = (z + r) % 8
        for e in range(2):
            if r == 0 and e == 0:
                continue
            to = core if e == 0 else other
            s = r * 2 + e
            start(remote(corr.at[zz, to], fz.at[s], fsend.at[s], frecv.at[s], devx(x, y, zz, to)))
    for k in range(4):
        both_cores(1, k)

    hwait(4, mext.at[pl.ds(0, 16), other])
    hwait(5, mext.at[pl.ds(16, 2), core])
    hwait(6, mext.at[pl.ds(16, 2), other])
    mx[0:1024] = mext[0:16].reshape(1024, 128).astype(F32)
    last = jnp.where(z == 7, 0.0, 1.0)
    mx[1024:1152] = mext[16:18].reshape(128, 128).astype(F32) * last

    def back_pair(i, _):
        r0, r1, base = rows_of(i)

        def taps8(jo, carry):
            m0, m1 = carry
            j0 = pl.multiple_of(jo * 8, 8)
            tap = taps[pl.ds(j0, 8), :]
            for ji in range(8):
                f = tap[ji:ji + 1, :]
                m0 = m0 + f * mx[pl.ds(base + j0 + ji, 32), :]
                m1 = m1 + f * mx[pl.ds(base + 64 + j0 + ji, 32), :]
            return m0, m1

        both = lax.fori_loop(0, 16, taps8, (zero, zero))
        for n, rows in enumerate((r0, r1)):
            gfb[i, 0, n] = (qkvg[3, rows, :].astype(F32) * acc[rows, 0:128]).astype(BF)
            gfb[i, 1, n] = (both[n] * qkvg[2, rows, :].astype(F32)).astype(BF)
            gfb[i, 2, n] = (both[n] * qkvg[1, rows, :].astype(F32)).astype(BF)
        return 0

    def gf_place(ysrc, csrc):
        return gfo.at[:, :, csrc, :, pl.ds(pl.multiple_of(ysrc * 128, 128), 128)]

    def gf_copy(i):
        return remote(
            gfb.at[i], gf_place(y, core), gsend.at[i], grecv.at[y * 2 + core], dev(xh, i % 2, i // 2, z, xl)
        )

    def gf_self(i):
        return jnp.logical_and(same, jnp.logical_and(y == i // 2, xl == i % 2))

    gf_local = pltpu.make_async_copy(gfb.at[y * 2 + xl], gf_place(y, core), lsem.at[13])
    for i in range(0, 8, 2):
        lax.fori_loop(i, i + 2, back_pair, 0)
        for n in (i, i + 1):
            @pl.when(gf_self(n))
            def _():
                gf_local.start()

            @pl.when(jnp.logical_not(gf_self(n)))
            def _():
                gf_copy(n).start()

    fs = corr[z, core]
    for s in range(1, 16):
        remote(fz.at[s], fz.at[s], fsend.at[s], frecv.at[s], partner).wait_recv()
        fs = fs + fz[s]
    ftot[...] = fs * scale
    fin_local = pltpu.make_async_copy(ftot, fin.at[y, core], lsem.at[14])

    def f_copy(i):
        return remote(
            ftot, fin.at[y, core], fsend.at[16 + i], frecv.at[16 + y * 2 + core], dev(xh, i % 2, i // 2, z, xl)
        )

    @pl.when(same)
    def _():
        fin_local.start()

    for i in range(8):
        @pl.when(jnp.logical_not(gf_self(i)))
        def _():
            f_copy(i).start()

    total = down[7]
    for i in range(7):
        remote(zbuf.at[i], zbuf.at[i], asend.at[i], arecv.at[i], partner).wait_recv()
        total = total + zbuf[i].astype(F32)
    tbuf[...] = (total.T * scale).reshape(4, 64, 128)

    def dw_place(ysrc):
        return dw_out.at[:, pl.ds(pl.multiple_of(ysrc * 128, 128), 128)]

    def dw_copy(k):
        yp, xp = core * 2 + k // 2, k % 2
        return remote(tbuf.at[k], dw_place(y), osend.at[k], orecv.at[y], dev(xh, xp, yp, z, xl))

    dw_here = jnp.logical_and(same, y // 2 == core)

    def dw_self(k):
        return jnp.logical_and(dw_here, jnp.logical_and(y % 2 == k // 2, xl == k % 2))

    dw_local = pltpu.make_async_copy(tbuf.at[(y % 2) * 2 + xl], dw_place(y), lsem.at[15])

    @pl.when(dw_here)
    def _():
        dw_local.start()

    for k in range(4):
        @pl.when(jnp.logical_not(dw_self(k)))
        def _():
            dw_copy(k).start()

    @pl.when(same)
    def _():
        fin_local.wait()

    for ys in range(4):
        for cs in range(2):
            me = jnp.logical_and(same, jnp.logical_and(y == ys, core == cs))

            @pl.when(jnp.logical_not(me))
            def _():
                s = 16 + ys * 2 + cs
                blk = fin.at[ys, cs]
                remote(blk, blk, fsend.at[s], frecv.at[s], partner).wait_recv()
    for r in range(1, 8):
        start(remote(fin, fout.at[z], fsend.at[24 + r], frecv.at[24 + r], devx(x, y, (z + r) % 8, core)))
    fout[z] = fin[...]

    @pl.when(dw_here)
    def _():
        dw_local.wait()

    for ys in range(4):
        @pl.when(jnp.logical_not(jnp.logical_and(dw_here, y == ys)))
        def _():
            blk = dw_place(ys)
            remote(blk, blk, osend.at[ys], orecv.at[ys], partner).wait_recv()

    @pl.when(same)
    def _():
        gf_local.wait()

    for ys in range(4):
        for cs in range(2):
            me = jnp.logical_and(same, jnp.logical_and(y == ys, core == cs))

            @pl.when(jnp.logical_not(me))
            def _():
                blk = gf_place(ys, cs)
                remote(blk, blk, gsend.at[0], grecv.at[ys * 2 + cs], partner).wait_recv()

    for r in range(1, 8):
        blk = fout.at[(z + 8 - r) % 8]
        remote(blk, blk, fsend.at[24 + r], frecv.at[24 + r], partner).wait_recv()
    for ys in range(4):
        fo[ys * 128:(ys + 1) * 128, :] = fout[:, ys].reshape(128, 128).T

    xs.finish()
    ga.finish()
    gb.finish()
    for c in sent:
        c.wait_send()
    for i in range(8):
        @pl.when(jnp.logical_not(gf_self(i)))
        def _():
            gf_copy(i).wait_send()
            f_copy(i).wait_send()
    for k in range(4):
        @pl.when(jnp.logical_not(dw_self(k)))
        def _():
            dw_copy(k).wait_send()


VM = pl.BlockSpec(memory_space=pltpu.VMEM)
HBM = pl.BlockSpec(memory_space=pltpu.HBM)
DMA = pltpu.SemaphoreType.DMA


def sds(shape, dtype):
    return jax.ShapeDtypeStruct(shape, dtype)


def on_device(block_input, featurizer, filters, out_weight, grad_output):
    scale = 1.0 / math.sqrt(128 * lax.axis_size("ctx"))
    gf, dw, gfilt = pl.pallas_call(
        functools.partial(block_kernel, scale),
        out_shape=(sds((3, 2, 2, 32, 512), BF), sds((64, 512), F32), sds((512, 128), F32)),
        in_specs=[HBM] * 5,
        out_specs=(VM, VM, VM),
        scratch_shapes=[
            pltpu.VMEM((4, 4, 32, 4096), BF),
            pltpu.VMEM((2, 4, 4, 4, 32, 512), BF),
            pltpu.VMEM((8, 4, 4, 2, 64, 128), BF),
            pltpu.VMEM((4, 64, 512), BF),
            pltpu.VMEM((128, 128), BF),
            pltpu.VMEM((128, 128), BF),
            pltpu.VMEM((512, 512), F32),
            pltpu.VMEM((4, 512, 128), BF),
            pltpu.VMEM((18, 2, 32, 128), BF),
            pltpu.VMEM((18, 2, 32, 128), BF),
            pltpu.VMEM((1152, 128), F32),
            pltpu.VMEM((1152, 128), F32),
            pltpu.VMEM((128, 128), F32),
            pltpu.VMEM((128, 8, 128), F32),
            pltpu.VMEM((8, 2, 8, 128), F32),
            pltpu.VMEM((128, 512), BF),
            pltpu.VMEM((8, 3, 2, 32, 128), BF),
            pltpu.VMEM((8, 128, 256), BF),
            pltpu.VMEM((8, 128, 256), F32),
            pltpu.VMEM((8, 128, 256), BF),
            pltpu.VMEM((7, 128, 256), BF),
            pltpu.VMEM((7, 128, 256), BF),
            pltpu.VMEM((4, 64, 128), F32),
            pltpu.VMEM((16, 8, 128), F32),
            pltpu.VMEM((8, 128), F32),
            pltpu.VMEM((4, 2, 8, 128), F32),
            pltpu.VMEM((8, 4, 2, 8, 128), F32),
            DMA((120,)), DMA((120,)), DMA((20,)), DMA((20,)), DMA((7,)), DMA((7,)), DMA((8,)), DMA((8,)),
            DMA((8,)), DMA((8,)), DMA((7,)), DMA((7,)), DMA((4,)), DMA((4,)), DMA((32,)), DMA((32,)),
            DMA((16,)),
        ],
        compiler_params=pltpu.CompilerParams(
            collective_id=1, has_side_effects=True, vmem_limit_bytes=40 * 2**20
        ),
        name="hyena_block",
    )(block_input, grad_output, featurizer.transpose(1, 0, 2), out_weight, filters)
    return gf.reshape(3, 128, 512).transpose(1, 0, 2), dw, gfilt


def solution(mesh):
    placed = (
        P(("ctx", "tp"), None),
        P("ctx", None, "tp"),
        P("tp", None),
        P("ctx", "tp"),
        P(("ctx", "tp"), None),
    )
    return jax.shard_map(
        on_device,
        mesh=mesh,
        in_specs=placed,
        out_specs=(P("ctx", None, "tp"), P("ctx", "tp"), P("tp", None)),
        check_vma=False,
    )
```

time: 116 us -> 105 us (0.905)
  Pallas kernels: 105 us -> 96.2 us
  local copies, waits for them, and re-layouts: 7.96 us -> 6.67 us
    pallas_call x3 -> x1, Pallas kernels: 105 us -> 96.2 us  [on_device(): pl.pallas_call(functools.partial(block_kernel, scale), out_shape=(sds((3,...]
    reshape x7 -> x0, local copies, waits for them, and re-layouts: 4.14 us -> none  [the longest x2 1.15 us: on_device(): f4 = featurizer.reshape(64, 3, 4, 128)]
    unnamed x7 -> x13, local copies, waits for them, and re-layouts: 3.41 us -> 6.67 us
where the time goes in v2:
time: 105 us; the launch traced here: 103 us
  Pallas kernels  96.2 us (92%)
  local copies, waits for them, and re-layouts  6.67 us (6%)
    pallas_call x1, Pallas kernels, on_device(): pl.pallas_call(functools.partial(block_kernel, scale), out_shape=(sds((3,...  96.2 us
    unnamed x13, local copies, waits for them, and re-layouts  6.67 us

profile of v2, /device:TPU:4, one launch (start us, length us, event | category | flops | bytes accessed | tf_op | source)
XLA Modules:
  0.0 103.5 jit_solution(12349084228588916080)
XLA Ops:
  0.6 0.0 copy-start
  0.6 0.9 copy-done
  1.6 0.0 copy-start.1
  1.6 0.9 copy-done.1
  2.5 0.0 copy-start.2
  2.5 0.9 copy-done.2
  3.5 0.0 copy-start.3
  3.5 0.9 copy-done.3
  4.4 0.0 copy-start.4
  4.4 0.8 copy-done.4
  5.2 96.2 %hyena_block.1 = (bf16[3,2,2,32,512]{4,3,2,1,0:T(8,128)(2,1)S(1)}, f32[64,512]{1,0:T(8,128)S(1)}, f32[512,128]{1,0:T(8,128)S(1)}) custom-call(bf16[32,4096]{1,0:T(8,128)(2,1)S(1)} %copy-done, bf16[32,4096]{1,0:T(8,128)(2,1)S(1)} %copy-done.1, bf16[3,64,512]{2,1,0:T(8,128)(2,1)S(1)} %bitcast.5, bf16[64,512]{1,0:T(8,128)(2,1)S(1)} %copy-done.4, ...), custom_call_target="tpu_custom_call" | custom-call | tf_op jit(solution)/shard_map/hyena_block/pallas_call | solution.py:621
  101.4 0.7 copy.11
  102.1 0.7 copy.12
  102.8 0.7 copy.13
Async XLA Ops:
  0.6 1.0 copy-start
  1.6 0.9 copy-start.1
  2.5 0.9 copy-start.2
  3.5 0.9 copy-start.3
  4.4 0.8 copy-start.4

commit v3 on v2

--- a/solution.py
+++ b/solution.py
@@ -124,7 +124,7 @@
     x_ref, g_ref, f_ref, w_ref, filt_ref,
     gfo, dw_out, fo,
     xbuf, gbuf, wbuf, wst, fst, filt_recv, acc, qkvg, gext, mext, gx, mx, taps, corr_acc, corr, mo,
-    gfb, dsend_buf, down, pbuf, sbuf, zbuf, tbuf, fz, ftot, fin, fout,
+    gfb, dsend_buf, down, pbuf, sbuf, zbuf, tbuf, fz, ftot, fin, finb, fout,
     psend, precv, wsend, wrecv, hsend, hrecv, gsend, grecv, dsend, drecv, asend, arecv, osend, orecv, fsend, frecv,
     lsem,
 ):
@@ -213,9 +213,9 @@
     def _():
         own_remote.start()
 
+    xs.step1()
     filt_copy = remote(fst, filt_recv, hsend.at[0], hrecv.at[0], partner)
     start(filt_copy)
-    xs.step1()
 
     def wblock(zrel, kinds=None, e=None):
         e = core if e is None else e
@@ -238,55 +238,52 @@
         blk = wblock(zrel, None, other)
         remote(blk, blk, wsend.at[12 + zrel], wrecv.at[12 + zrel], partner).wait_recv()
 
-    @pl.when(same)
-    def _():
-        own_local.wait()
-
-    @pl.when(apart)
-    def _():
-        blk = wbuf.at[z, :, y, core]
-        own_remote.wait_send()
-        remote(blk, blk, wsend.at[0], wrecv.at[0], dev(xh, 1 - xl, y, z, other)).wait_recv()
-
-    for dy in (1, 2, 3):
-        blk = wbuf.at[z, :, (y + 4 - dy) % 4, core]
-        remote(blk, blk, wsend.at[dy], wrecv.at[dy], partner).wait_recv()
-
-    wring_send(4, 0, None, zp)
-    wring_send(8, 0, None, zm)
-    wpair_send(0)
+    def weights_in():
+        @pl.when(same)
+        def _():
+            own_local.wait()
+
+        @pl.when(apart)
+        def _():
+            blk = wbuf.at[z, :, y, core]
+            own_remote.wait_send()
+            remote(blk, blk, wsend.at[0], wrecv.at[0], dev(xh, 1 - xl, y, z, other)).wait_recv()
+
+        for dy in (1, 2, 3):
+            blk = wbuf.at[z, :, (y + 4 - dy) % 4, core]
+            remote(blk, blk, wsend.at[dy], wrecv.at[dy], partner).wait_recv()
+        wring_send(4, 0, None, zp)
+        wring_send(8, 0, None, zm)
+        wpair_send(0)
+
+    def weights_hop(n):
+        last = n == 3
+        wring_wait(3 + n, n, None)
+        wring_send(4 + n, n, 0 if last else None, zp)
+        wpair_send(n)
+        wring_wait(7 + n, 8 - n, None)
+        wring_send(8 + n, 8 - n, 2 if last else None, zm)
+        wpair_send(8 - n)
+
     xs.step2()
-    wring_wait(4, 1, None)
-    wring_send(5, 1, None, zp)
-    wpair_send(1)
-    wring_wait(8, 7, None)
-    wring_send(9, 7, None, zm)
-    wpair_send(7)
+    weights_in()
+    xs.step4(0)
     xs.step3()
-    xs.step4(0)
-    wring_wait(5, 2, None)
-    wring_send(6, 2, None, zp)
-    wpair_send(2)
-    wring_wait(9, 6, None)
-    wring_send(10, 6, None, zm)
-    wpair_send(6)
     ga.step1()
+    weights_hop(1)
     xs.step4(3)
     xs.step4(1)
-    wring_wait(6, 3, None)
-    wring_send(7, 3, 0, zp)
-    wpair_send(3)
-    wring_wait(10, 5, None)
-    wring_send(11, 5, 2, zm)
-    wpair_send(5)
+    weights_hop(2)
+    ga.step2()
     xs.step4(2)
-    ga.step2()
+    ga.step4(0)
+    weights_hop(3)
+    ga.step3()
     xs.step5()
+    gb.step1()
     wring_wait(7, 4, 0)
     wring_wait(11, 4, 2)
     wpair_send(4)
-    ga.step3()
-    ga.step4(0)
     for zrel in range(8):
         wpair_wait(zrel)
 
@@ -301,7 +298,6 @@
 
     lax.fori_loop(0, 4, project_x, 0)
     ga.step4(3)
-    gb.step1()
     lax.fori_loop(4, 8, project_x, 0)
     ga.step4(1)
 
@@ -316,8 +312,9 @@
     start(remote(own, own, hsend.at[1], hrecv.at[1], partner))
     start(remote(tail, head, hsend.at[2], hrecv.at[2], devx(x, y, zp, core)))
     start(remote(tail, head, hsend.at[3], hrecv.at[3], devx(x, y, zp, other)))
+    gb.step2()
     ga.step4(2)
-    gb.step2()
+    gb.step4(0)
     ga.step5()
 
     def project_g(h, k):
@@ -325,9 +322,8 @@
         rhs = wbuf[(z + FAR[h][k]) % 8, 3].reshape(512, 128)
         return jnp.dot(lhs, rhs, preferred_element_type=F32)
 
-    acc[:, 384:512] = project_g(0, 0) + project_g(0, 1)
     gb.step3()
-    acc[:, 384:512] += project_g(0, 2) + project_g(0, 3)
+    acc[:, 384:512] = project_g(0, 0) + project_g(0, 1) + project_g(0, 2) + project_g(0, 3)
 
     filt_copy.wait_recv()
     mine = jnp.where(same, 1.0, 0.0)
@@ -342,7 +338,6 @@
     first = jnp.where(z == 0, 0.0, 1.0)
     gx[0:128] = gext[0:2].reshape(128, 128).astype(F32) * first
     gx[128:1152] = gext[2:18].reshape(1024, 128).astype(F32)
-    gb.step4(0)
 
     zero = jnp.zeros((32, 128), F32)
 
@@ -374,7 +369,6 @@
     gb.step4(1)
     lax.fori_loop(6, 8, mixed_pair, 0)
     mo[...] = (qkvg[0].astype(F32) * acc[:, 0:128]).T.astype(BF)
-    gb.step4(2)
 
     def grad_w(h, k):
         def term(e):
@@ -397,11 +391,11 @@
 
     for k in range(4):
         grad_w(0, k)
-    gb.step5()
-    acc[:, 384:512] += project_g(1, 0) + project_g(1, 1)
+    gb.step4(2)
     for k in range(4):
         both_cores(0, k)
-    acc[:, 384:512] += project_g(1, 2) + project_g(1, 3)
+    gb.step5()
+    acc[:, 384:512] += project_g(1, 0) + project_g(1, 1) + project_g(1, 2) + project_g(1, 3)
 
     qkvg[3] = acc[:, 384:512].astype(BF)
     gmixed = (qkvg[3].astype(F32) * qkvg[0].astype(F32)).astype(BF)
@@ -412,8 +406,6 @@
     start(remote(mown, mown, hsend.at[4], hrecv.at[4], partner))
     start(remote(mhead, mtail, hsend.at[5], hrecv.at[5], devx(x, y, zm, core)))
     start(remote(mhead, mtail, hsend.at[6], hrecv.at[6], devx(x, y, zm, other)))
-    for k in range(4):
-        grad_w(1, k)
 
     corr_acc[...] = jnp.zeros_like(corr_acc)
 
@@ -443,6 +435,8 @@
             s = r * 2 + e
             start(remote(corr.at[zz, to], fz.at[s], fsend.at[s], frecv.at[s], devx(x, y, zz, to)))
     for k in range(4):
+        grad_w(1, k)
+    for k in range(4):
         both_cores(1, k)
 
     hwait(4, mext.at[pl.ds(0, 16), other])
@@ -483,8 +477,33 @@
     def gf_self(i):
         return jnp.logical_and(same, jnp.logical_and(y == i // 2, xl == i % 2))
 
+    fin_local = pltpu.make_async_copy(ftot, fin.at[y, core], lsem.at[14])
+
+    def f_copy(i):
+        return remote(
+            ftot, fin.at[y, core], fsend.at[16 + i], frecv.at[16 + y * 2 + core], dev(xh, i % 2, i // 2, z, xl)
+        )
+
+    def filters_out():
+        fs = corr[z, core]
+        for s in range(1, 16):
+            remote(fz.at[s], fz.at[s], fsend.at[s], frecv.at[s], partner).wait_recv()
+            fs = fs + fz[s]
+        ftot[...] = fs * scale
+
+        @pl.when(same)
+        def _():
+            fin_local.start()
+
+        for i in range(8):
+            @pl.when(jnp.logical_not(gf_self(i)))
+            def _():
+                f_copy(i).start()
+
     gf_local = pltpu.make_async_copy(gfb.at[y * 2 + xl], gf_place(y, core), lsem.at[13])
     for i in range(0, 8, 2):
+        if i == 4:
+            filters_out()
         lax.fori_loop(i, i + 2, back_pair, 0)
         for n in (i, i + 1):
             @pl.when(gf_self(n))
@@ -495,27 +514,6 @@
             def _():
                 gf_copy(n).start()
 
-    fs = corr[z, core]
-    for s in range(1, 16):
-        remote(fz.at[s], fz.at[s], fsend.at[s], frecv.at[s], partner).wait_recv()
-        fs = fs + fz[s]
-    ftot[...] = fs * scale
-    fin_local = pltpu.make_async_copy(ftot, fin.at[y, core], lsem.at[14])
-
-    def f_copy(i):
-        return remote(
-            ftot, fin.at[y, core], fsend.at[16 + i], frecv.at[16 + y * 2 + core], dev(xh, i % 2, i // 2, z, xl)
-        )
-
-    @pl.when(same)
-    def _():
-        fin_local.start()
-
-    for i in range(8):
-        @pl.when(jnp.logical_not(gf_self(i)))
-        def _():
-            f_copy(i).start()
-
     total = down[7]
     for i in range(7):
         remote(zbuf.at[i], zbuf.at[i], asend.at[i], arecv.at[i], partner).wait_recv()
@@ -558,9 +556,10 @@
                 s = 16 + ys * 2 + cs
                 blk = fin.at[ys, cs]
                 remote(blk, blk, fsend.at[s], frecv.at[s], partner).wait_recv()
+    finb[...] = fin[...].reshape(4, 16, 128).astype(BF)
     for r in range(1, 8):
-        start(remote(fin, fout.at[z], fsend.at[24 + r], frecv.at[24 + r], devx(x, y, (z + r) % 8, core)))
-    fout[z] = fin[...]
+        start(remote(finb, fout.at[z], fsend.at[24 + r], frecv.at[24 + r], devx(x, y, (z + r) % 8, core)))
+    fout[z] = finb[...]
 
     @pl.when(dw_here)
     def _():
@@ -589,7 +588,7 @@
         blk = fout.at[(z + 8 - r) % 8]
         remote(blk, blk, fsend.at[24 + r], frecv.at[24 + r], partner).wait_recv()
     for ys in range(4):
-        fo[ys * 128:(ys + 1) * 128, :] = fout[:, ys].reshape(128, 128).T
+        fo[ys * 128:(ys + 1) * 128, :] = fout[:, ys].reshape(128, 128).astype(F32).T
 
     xs.finish()
     ga.finish()
@@ -650,13 +649,14 @@
             pltpu.VMEM((16, 8, 128), F32),
             pltpu.VMEM((8, 128), F32),
             pltpu.VMEM((4, 2, 8, 128), F32),
-            pltpu.VMEM((8, 4, 2, 8, 128), F32),
+            pltpu.VMEM((4, 16, 128), BF),
+            pltpu.VMEM((8, 4, 16, 128), BF),
             DMA((120,)), DMA((120,)), DMA((20,)), DMA((20,)), DMA((7,)), DMA((7,)), DMA((8,)), DMA((8,)),
             DMA((8,)), DMA((8,)), DMA((7,)), DMA((7,)), DMA((4,)), DMA((4,)), DMA((32,)), DMA((32,)),
             DMA((16,)),
         ],
         compiler_params=pltpu.CompilerParams(
-            collective_id=1, has_side_effects=True, vmem_limit_bytes=40 * 2**20
+            collective_id=1, has_side_effects=True, vmem_limit_bytes=60 * 2**20
         ),
         name="hyena_block",
     )(block_input, grad_output, featurizer.transpose(1, 0, 2), out_weight, filters)

time: 105 us -> 97.6 us (0.930)
  Pallas kernels: 96.2 us -> 92.8 us
  local copies, waits for them, and re-layouts: 6.67 us -> 3.5 us
    pallas_call x1, Pallas kernels: 96.2 us -> 92.8 us  [on_device(): pl.pallas_call(functools.partial(block_kernel, scale), out_shape=(sds((3,...]
    unnamed x13 -> x7, local copies, waits for them, and re-layouts: 6.67 us -> 3.5 us
where the time goes in v3:
time: 97.6 us; the launch traced here: 97 us
  Pallas kernels  92.8 us (95%)
  local copies, waits for them, and re-layouts  3.5 us (4%)
    pallas_call x1, Pallas kernels, on_device(): pl.pallas_call(functools.partial(block_kernel, scale), out_shape=(sds((3,...  92.8 us
    unnamed x7, local copies, waits for them, and re-layouts  3.5 us

profile of v3, /device:TPU:4, one launch (start us, length us, event | category | flops | bytes accessed | tf_op | source)
XLA Modules:
  0.0 97.0 jit_solution(752995720182454979)
XLA Ops:
  0.6 92.8 %hyena_block.1 = (bf16[3,2,2,32,512]{4,3,2,1,0:T(8,128)(2,1)}, f32[64,512]{1,0:T(8,128)}, f32[512,128]{1,0:T(8,128)}) custom-call(bf16[32,4096]{1,0:T(8,128)(2,1)} %x_ref.1, bf16[32,4096]{1,0:T(8,128)(2,1)} %g_ref.1, bf16[3,64,512]{2,1,0:T(8,128)(2,1)} %bitcast.5, bf16[64,512]{1,0:T(8,128)(2,1)} %w_ref.1, bf16[512,128]{1,0:T(8,128)(2,1)} %filt_ref.1), custom_call_target="tpu_custom_call" | custom-call | tf_op jit(solution)/shard_map/hyena_block/pallas_call | solution.py:620
  93.5 0.0 copy-start.1
  93.5 1.8 %copy.11 = bf16[128,3,512]{2,0,1:T(8,128)(2,1)} copy(bf16[128,3,512]{2,0,1:T(8,128)(2,1)} %bitcast.4) | data formatting | bytes 786432
  95.3 0.0 copy-done.1
  95.3 0.0 copy-start
  95.3 0.7 copy.12
  96.0 0.3 copy-done
  96.3 0.7 copy.13
Async XLA Ops:
  93.5 1.8 %copy-start.1 = (f32[64,512]{1,0:T(8,128)S(1)}, f32[64,512]{1,0:T(8,128)}, u32[]{:S(2)}) copy-start(f32[64,512]{1,0:T(8,128)} %get-tuple-element.13) | copy-start | bytes 393220
  95.3 1.0 %copy-start = (f32[512,128]{1,0:T(8,128)S(1)}, f32[512,128]{1,0:T(8,128)}, u32[]{:S(2)}) copy-start(f32[512,128]{1,0:T(8,128)} %get-tuple-element.14) | copy-start | bytes 786436

commit v4 on v3

--- a/solution.py
+++ b/solution.py
@@ -145,18 +145,9 @@
         partner,
         dev(xh, 1 - xl, y, z, other),
     ] + [dev(xh, core, (y + dy) % 4, z, xl) for dy in (1, 2, 3)]
-    for r in range(1, 8):
-        greet += [devx(x, y, (z + r) % 8, core), devx(x, y, (z + r) % 8, other)]
+    greet += [devx(x, y, zp, core), devx(x, y, zm, core)]
     for d in greet:
         pl.semaphore_signal(barrier, inc=1, device_id=d, device_id_type=MESH)
-    for ys in range(4):
-        for cs in range(2):
-            me = jnp.logical_and(same, jnp.logical_and(y == ys, core == cs))
-
-            @pl.when(jnp.logical_not(me))
-            def _():
-                pl.semaphore_signal(barrier, inc=1, device_id=dev(xh, core, ys, z, cs), device_id_type=MESH)
-
     stage = [
         pltpu.make_async_copy(f_ref, wst.at[pl.ds(0, 3)], lsem.at[0]),
         pltpu.make_async_copy(w_ref, wst.at[3], lsem.at[1]),
@@ -173,7 +164,7 @@
         c.start()
     for c in stage:
         c.wait()
-    pl.semaphore_wait(barrier, len(greet) + 8 - jnp.where(same, 1, 0))
+    pl.semaphore_wait(barrier, len(greet))
 
     def place_x(yy, s, lr, half):
         cols = pl.ds(0, 4096) if half is None else pl.ds(half * 2048, 2048)
@@ -222,21 +213,23 @@
         zz = (z + 8 - zrel) % 8
         return wbuf.at[zz, :, :, e] if kinds is None else wbuf.at[zz, pl.ds(kinds, 2), :, e]
 
-    def wring_send(sem, zrel, kinds, to):
-        blk = wblock(zrel, kinds)
-        start(remote(blk, blk, wsend.at[sem], wrecv.at[sem], devx(x, y, to, core)))
-
-    def wring_wait(sem, zrel, kinds):
-        blk = wblock(zrel, kinds)
-        remote(blk, blk, wsend.at[sem], wrecv.at[sem], devx(x, y, zp, core)).wait_recv()
+    def wring_send(plus, hop, piece):
+        blk = wblock(hop - 1 if plus else (9 - hop) % 8, piece * 2)
+        n = 4 + (0 if plus else 8) + (hop - 1) * 2 + piece
+        start(remote(blk, blk, wsend.at[n], wrecv.at[n], devx(x, y, zp if plus else zm, core)))
+
+    def wring_wait(plus, hop, piece):
+        blk = wblock(hop if plus else 8 - hop, piece * 2)
+        n = 4 + (0 if plus else 8) + (hop - 1) * 2 + piece
+        remote(blk, blk, wsend.at[n], wrecv.at[n], devx(x, y, zp, core)).wait_recv()
 
     def wpair_send(zrel):
         blk = wblock(zrel)
-        start(remote(blk, blk, wsend.at[12 + zrel], wrecv.at[12 + zrel], partner))
+        start(remote(blk, blk, wsend.at[20 + zrel], wrecv.at[20 + zrel], partner))
 
     def wpair_wait(zrel):
         blk = wblock(zrel, None, other)
-        remote(blk, blk, wsend.at[12 + zrel], wrecv.at[12 + zrel], partner).wait_recv()
+        remote(blk, blk, wsend.at[20 + zrel], wrecv.at[20 + zrel], partner).wait_recv()
 
     def weights_in():
         @pl.when(same)
@@ -252,18 +245,21 @@
         for dy in (1, 2, 3):
             blk = wbuf.at[z, :, (y + 4 - dy) % 4, core]
             remote(blk, blk, wsend.at[dy], wrecv.at[dy], partner).wait_recv()
-        wring_send(4, 0, None, zp)
-        wring_send(8, 0, None, zm)
+        for piece in range(2):
+            wring_send(True, 1, piece)
+            wring_send(False, 1, piece)
         wpair_send(0)
 
     def weights_hop(n):
-        last = n == 3
-        wring_wait(3 + n, n, None)
-        wring_send(4 + n, n, 0 if last else None, zp)
+        for piece in range(2):
+            for plus in (True, False):
+                if n < 4 or plus == (piece == 0):
+                    wring_wait(plus, n, piece)
+                    if n < 3 or (n == 3 and plus == (piece == 0)):
+                        wring_send(plus, n + 1, piece)
         wpair_send(n)
-        wring_wait(7 + n, 8 - n, None)
-        wring_send(8 + n, 8 - n, 2 if last else None, zm)
-        wpair_send(8 - n)
+        if n < 4:
+            wpair_send(8 - n)
 
     xs.step2()
     weights_in()
@@ -272,18 +268,16 @@
     ga.step1()
     weights_hop(1)
     xs.step4(3)
+    weights_hop(2)
     xs.step4(1)
-    weights_hop(2)
+    xs.step4(2)
+    weights_hop(3)
+    xs.step5()
     ga.step2()
-    xs.step4(2)
+    weights_hop(4)
     ga.step4(0)
-    weights_hop(3)
     ga.step3()
-    xs.step5()
     gb.step1()
-    wring_wait(7, 4, 0)
-    wring_wait(11, 4, 2)
-    wpair_send(4)
     for zrel in range(8):
         wpair_wait(zrel)
 
@@ -299,7 +293,6 @@
     lax.fori_loop(0, 4, project_x, 0)
     ga.step4(3)
     lax.fori_loop(4, 8, project_x, 0)
-    ga.step4(1)
 
     for i in range(3):
         qkvg[i] = acc[:, i * 128:(i + 1) * 128].astype(BF)
@@ -312,18 +305,16 @@
     start(remote(own, own, hsend.at[1], hrecv.at[1], partner))
     start(remote(tail, head, hsend.at[2], hrecv.at[2], devx(x, y, zp, core)))
     start(remote(tail, head, hsend.at[3], hrecv.at[3], devx(x, y, zp, other)))
+    ga.step4(1)
+    xs.finish()
     gb.step2()
     ga.step4(2)
     gb.step4(0)
-    ga.step5()
 
     def project_g(h, k):
         lhs = gbuf[h, :, :, k].reshape(512, 512)
         rhs = wbuf[(z + FAR[h][k]) % 8, 3].reshape(512, 128)
         return jnp.dot(lhs, rhs, preferred_element_type=F32)
-
-    gb.step3()
-    acc[:, 384:512] = project_g(0, 0) + project_g(0, 1) + project_g(0, 2) + project_g(0, 3)
 
     filt_copy.wait_recv()
     mine = jnp.where(same, 1.0, 0.0)
@@ -363,12 +354,12 @@
         acc[r1, 0:128] = m1
         return 0
 
-    lax.fori_loop(0, 3, mixed_pair, 0)
+    lax.fori_loop(0, 4, mixed_pair, 0)
+    gb.step3()
+    lax.fori_loop(4, 8, mixed_pair, 0)
+    mo[...] = (qkvg[0].astype(F32) * acc[:, 0:128]).T.astype(BF)
+    ga.step5()
     gb.step4(3)
-    lax.fori_loop(3, 6, mixed_pair, 0)
-    gb.step4(1)
-    lax.fori_loop(6, 8, mixed_pair, 0)
-    mo[...] = (qkvg[0].astype(F32) * acc[:, 0:128]).T.astype(BF)
 
     def grad_w(h, k):
         def term(e):
@@ -391,9 +382,12 @@
 
     for k in range(4):
         grad_w(0, k)
-    gb.step4(2)
+    gb.step4(1)
     for k in range(4):
         both_cores(0, k)
+    acc[:, 384:512] = project_g(0, 0) + project_g(0, 1) + project_g(0, 2) + project_g(0, 3)
+    gb.step4(2)
+    ga.finish()
     gb.step5()
     acc[:, 384:512] += project_g(1, 0) + project_g(1, 1) + project_g(1, 2) + project_g(1, 3)
 
@@ -584,14 +578,6 @@
                 blk = gf_place(ys, cs)
                 remote(blk, blk, gsend.at[0], grecv.at[ys * 2 + cs], partner).wait_recv()
 
-    for r in range(1, 8):
-        blk = fout.at[(z + 8 - r) % 8]
-        remote(blk, blk, fsend.at[24 + r], frecv.at[24 + r], partner).wait_recv()
-    for ys in range(4):
-        fo[ys * 128:(ys + 1) * 128, :] = fout[:, ys].reshape(128, 128).astype(F32).T
-
-    xs.finish()
-    ga.finish()
     gb.finish()
     for c in sent:
         c.wait_send()
@@ -605,6 +591,11 @@
         def _():
             dw_copy(k).wait_send()
 
+    for r in range(1, 8):
+        blk = fout.at[(z + 8 - r) % 8]
+        remote(blk, blk, fsend.at[24 + r], frecv.at[24 + r], partner).wait_recv()
+    for ys in range(4):
+        fo[ys * 128:(ys + 1) * 128, :] = fout[:, ys].reshape(128, 128).astype(F32).T
 
 VM = pl.BlockSpec(memory_space=pltpu.VMEM)
 HBM = pl.BlockSpec(memory_space=pltpu.HBM)
@@ -651,7 +642,7 @@
             pltpu.VMEM((4, 2, 8, 128), F32),
             pltpu.VMEM((4, 16, 128), BF),
             pltpu.VMEM((8, 4, 16, 128), BF),
-            DMA((120,)), DMA((120,)), DMA((20,)), DMA((20,)), DMA((7,)), DMA((7,)), DMA((8,)), DMA((8,)),
+            DMA((120,)), DMA((120,)), DMA((28,)), DMA((28,)), DMA((7,)), DMA((7,)), DMA((8,)), DMA((8,)),
             DMA((8,)), DMA((8,)), DMA((7,)), DMA((7,)), DMA((4,)), DMA((4,)), DMA((32,)), DMA((32,)),
             DMA((16,)),
         ],

time: 97.6 us -> 94.3 us (0.966)
  Pallas kernels: 92.8 us -> 88.9 us
    pallas_call x1, Pallas kernels: 92.8 us -> 88.9 us  [on_device(): pl.pallas_call(functools.partial(block_kernel, scale), out_shape=(sds((3,...]
where the time goes in v4:
time: 94.3 us; the launch traced here: 93 us
  Pallas kernels  88.9 us (94%)
  local copies, waits for them, and re-layouts  3.5 us (4%)
    pallas_call x1, Pallas kernels, on_device(): pl.pallas_call(functools.partial(block_kernel, scale), out_shape=(sds((3,...  88.9 us
    unnamed x7, local copies, waits for them, and re-layouts  3.5 us

profile of v4, /device:TPU:4, one launch (start us, length us, event | category | flops | bytes accessed | tf_op | source)
XLA Modules:
  0.0 93.0 jit_solution(16204261209201114948)
XLA Ops:
  0.6 88.9 %hyena_block.1 = (bf16[3,2,2,32,512]{4,3,2,1,0:T(8,128)(2,1)}, f32[64,512]{1,0:T(8,128)}, f32[512,128]{1,0:T(8,128)}) custom-call(bf16[32,4096]{1,0:T(8,128)(2,1)} %x_ref.1, bf16[32,4096]{1,0:T(8,128)(2,1)} %g_ref.1, bf16[3,64,512]{2,1,0:T(8,128)(2,1)} %bitcast.5, bf16[64,512]{1,0:T(8,128)(2,1)} %w_ref.1, bf16[512,128]{1,0:T(8,128)(2,1)} %filt_ref.1), custom_call_target="tpu_custom_call" | custom-call | tf_op jit(solution)/shard_map/hyena_block/pallas_call | solution.py:611
  89.5 0.0 copy-start.1
  89.5 1.8 %copy.11 = bf16[128,3,512]{2,0,1:T(8,128)(2,1)} copy(bf16[128,3,512]{2,0,1:T(8,128)(2,1)} %bitcast.4) | data formatting | bytes 786432
  91.3 0.0 copy-done.1
  91.3 0.0 copy-start
  91.3 0.7 copy.12
  92.0 0.3 copy-done
  92.3 0.7 copy.13
Async XLA Ops:
  89.5 1.8 %copy-start.1 = (f32[64,512]{1,0:T(8,128)S(1)}, f32[64,512]{1,0:T(8,128)}, u32[]{:S(2)}) copy-start(f32[64,512]{1,0:T(8,128)} %get-tuple-element.13) | copy-start | bytes 393220
  91.3 1.0 %copy-start = (f32[512,128]{1,0:T(8,128)S(1)}, f32[512,128]{1,0:T(8,128)}, u32[]{:S(2)}) copy-start(f32[512,128]{1,0:T(8,128)} %get-tuple-element.14) | copy-start | bytes 786436

commit v5 on v4

--- a/solution.py
+++ b/solution.py
@@ -262,22 +262,22 @@
             wpair_send(8 - n)
 
     xs.step2()
+    xs.step4(0)
     weights_in()
-    xs.step4(0)
     xs.step3()
     ga.step1()
+    xs.step4(3)
     weights_hop(1)
-    xs.step4(3)
+    xs.step4(1)
     weights_hop(2)
-    xs.step4(1)
     xs.step4(2)
+    ga.step2()
     weights_hop(3)
+    ga.step4(0)
     xs.step5()
-    ga.step2()
-    weights_hop(4)
-    ga.step4(0)
     ga.step3()
     gb.step1()
+    weights_hop(4)
     for zrel in range(8):
         wpair_wait(zrel)
 
@@ -306,10 +306,10 @@
     start(remote(tail, head, hsend.at[2], hrecv.at[2], devx(x, y, zp, core)))
     start(remote(tail, head, hsend.at[3], hrecv.at[3], devx(x, y, zp, other)))
     ga.step4(1)
-    xs.finish()
     gb.step2()
     ga.step4(2)
     gb.step4(0)
+    xs.finish()
 
     def project_g(h, k):
         lhs = gbuf[h, :, :, k].reshape(512, 512)

time: 94.3 us -> 92.7 us (0.983)
  Pallas kernels: 88.9 us -> 87.4 us
    pallas_call x1, Pallas kernels: 88.9 us -> 87.4 us  [on_device(): pl.pallas_call(functools.partial(block_kernel, scale), out_shape=(sds((3,...]
where the time goes in v5:
time: 92.7 us; the launch traced here: 91.5 us
  Pallas kernels  87.4 us (94%)
  local copies, waits for them, and re-layouts  3.5 us (4%)
    pallas_call x1, Pallas kernels, on_device(): pl.pallas_call(functools.partial(block_kernel, scale), out_shape=(sds((3,...  87.4 us
    unnamed x7, local copies, waits for them, and re-layouts  3.5 us

profile of v5, /device:TPU:4, one launch (start us, length us, event | category | flops | bytes accessed | tf_op | source)
XLA Modules:
  0.0 91.5 jit_solution(17551782785455597275)
XLA Ops:
  0.6 87.4 %hyena_block.1 = (bf16[3,2,2,32,512]{4,3,2,1,0:T(8,128)(2,1)}, f32[64,512]{1,0:T(8,128)}, f32[512,128]{1,0:T(8,128)}) custom-call(bf16[32,4096]{1,0:T(8,128)(2,1)} %x_ref.1, bf16[32,4096]{1,0:T(8,128)(2,1)} %g_ref.1, bf16[3,64,512]{2,1,0:T(8,128)(2,1)} %bitcast.5, bf16[64,512]{1,0:T(8,128)(2,1)} %w_ref.1, bf16[512,128]{1,0:T(8,128)(2,1)} %filt_ref.1), custom_call_target="tpu_custom_call" | custom-call | tf_op jit(solution)/shard_map/hyena_block/pallas_call | solution.py:611
  88.0 0.0 copy-start.1
  88.0 1.8 %copy.11 = bf16[128,3,512]{2,0,1:T(8,128)(2,1)} copy(bf16[128,3,512]{2,0,1:T(8,128)(2,1)} %bitcast.4) | data formatting | bytes 786432
  89.8 0.0 copy-done.1
  89.8 0.0 copy-start
  89.8 0.7 copy.12
  90.5 0.3 copy-done
  90.8 0.7 copy.13
Async XLA Ops:
  88.0 1.8 %copy-start.1 = (f32[64,512]{1,0:T(8,128)S(1)}, f32[64,512]{1,0:T(8,128)}, u32[]{:S(2)}) copy-start(f32[64,512]{1,0:T(8,128)} %get-tuple-element.13) | copy-start | bytes 393220
  89.8 1.0 %copy-start = (f32[512,128]{1,0:T(8,128)S(1)}, f32[512,128]{1,0:T(8,128)}, u32[]{:S(2)}) copy-start(f32[512,128]{1,0:T(8,128)} %get-tuple-element.14) | copy-start | bytes 786436

commit v6 on v5

--- a/solution.py
+++ b/solution.py
@@ -277,22 +277,24 @@
     xs.step5()
     ga.step3()
     gb.step1()
+
+    def project_x(zrels, fresh=False):
+        total = None if fresh else acc[:, 0:384]
+        for zrel in zrels:
+            wpair_wait(zrel)
+            i = (z + 8 - zrel) % 8
+            cols = pl.ds(pl.multiple_of(i * 512, 512), 512)
+            lhs = xbuf[:, :, :, cols].reshape(512, 512)
+            rhs = jnp.concatenate([wbuf[i, kind].reshape(512, 128) for kind in range(3)], axis=1)
+            term = jnp.dot(lhs, rhs, preferred_element_type=F32)
+            total = term if total is None else total + term
+        acc[:, 0:384] = total
+
+    project_x((0, 1, 7), True)
     weights_hop(4)
-    for zrel in range(8):
-        wpair_wait(zrel)
-
-    acc[...] = jnp.zeros_like(acc)
-
-    def project_x(i, _):
-        cols = pl.ds(pl.multiple_of(i * 512, 512), 512)
-        lhs = xbuf[:, :, :, cols].reshape(512, 512)
-        rhs = jnp.concatenate([wbuf[i, kind].reshape(512, 128) for kind in range(3)], axis=1)
-        acc[:, 0:384] += jnp.dot(lhs, rhs, preferred_element_type=F32)
-        return 0
-
-    lax.fori_loop(0, 4, project_x, 0)
+    project_x((2, 6))
     ga.step4(3)
-    lax.fori_loop(4, 8, project_x, 0)
+    project_x((3, 5, 4))
 
     for i in range(3):
         qkvg[i] = acc[:, i * 128:(i + 1) * 128].astype(BF)

time: 92.7 us -> 89.9 us (0.970)
  Pallas kernels: 87.4 us -> 85.5 us
    pallas_call x1, Pallas kernels: 87.4 us -> 85.5 us  [on_device(): pl.pallas_call(functools.partial(block_kernel, scale), out_shape=(sds((3,...]
where the time goes in v6:
time: 89.9 us; the launch traced here: 89.6 us
  Pallas kernels  85.5 us (95%)
  local copies, waits for them, and re-layouts  3.5 us (4%)
    pallas_call x1, Pallas kernels, on_device(): pl.pallas_call(functools.partial(block_kernel, scale), out_shape=(sds((3,...  85.5 us
    unnamed x7, local copies, waits for them, and re-layouts  3.5 us

profile of v6, /device:TPU:4, one launch (start us, length us, event | category | flops | bytes accessed | tf_op | source)
XLA Modules:
  0.0 89.6 jit_solution(6734487790685877932)
XLA Ops:
  0.6 85.5 %hyena_block.1 = (bf16[3,2,2,32,512]{4,3,2,1,0:T(8,128)(2,1)}, f32[64,512]{1,0:T(8,128)}, f32[512,128]{1,0:T(8,128)}) custom-call(bf16[32,4096]{1,0:T(8,128)(2,1)} %x_ref.1, bf16[32,4096]{1,0:T(8,128)(2,1)} %g_ref.1, bf16[3,64,512]{2,1,0:T(8,128)(2,1)} %bitcast.5, bf16[64,512]{1,0:T(8,128)(2,1)} %w_ref.1, bf16[512,128]{1,0:T(8,128)(2,1)} %filt_ref.1), custom_call_target="tpu_custom_call" | custom-call | tf_op jit(solution)/shard_map/hyena_block/pallas_call | solution.py:613
  86.1 0.0 copy-start.1
  86.1 1.8 %copy.11 = bf16[128,3,512]{2,0,1:T(8,128)(2,1)} copy(bf16[128,3,512]{2,0,1:T(8,128)(2,1)} %bitcast.4) | data formatting | bytes 786432
  87.9 0.0 copy-done.1
  87.9 0.0 copy-start
  87.9 0.7 copy.12
  88.6 0.3 copy-done
  88.9 0.7 copy.13
Async XLA Ops:
  86.1 1.8 %copy-start.1 = (f32[64,512]{1,0:T(8,128)S(1)}, f32[64,512]{1,0:T(8,128)}, u32[]{:S(2)}) copy-start(f32[64,512]{1,0:T(8,128)} %get-tuple-element.13) | copy-start | bytes 393220
  87.9 1.0 %copy-start = (f32[512,128]{1,0:T(8,128)S(1)}, f32[512,128]{1,0:T(8,128)}, u32[]{:S(2)}) copy-start(f32[512,128]{1,0:T(8,128)} %get-tuple-element.14) | copy-start | bytes 786436

commit v7 on v6

--- a/solution.py
+++ b/solution.py
@@ -387,8 +387,8 @@
     gb.step4(1)
     for k in range(4):
         both_cores(0, k)
+    gb.step4(2)
     acc[:, 384:512] = project_g(0, 0) + project_g(0, 1) + project_g(0, 2) + project_g(0, 3)
-    gb.step4(2)
     ga.finish()
     gb.step5()
     acc[:, 384:512] += project_g(1, 0) + project_g(1, 1) + project_g(1, 2) + project_g(1, 3)
@@ -498,7 +498,7 @@
 
     gf_local = pltpu.make_async_copy(gfb.at[y * 2 + xl], gf_place(y, core), lsem.at[13])
     for i in range(0, 8, 2):
-        if i == 4:
+        if i == 2:
             filters_out()
         lax.fori_loop(i, i + 2, back_pair, 0)
         for n in (i, i + 1):

time: 89.9 us -> 89.4 us (level)
  no operation moved by 1% of the time
where the time goes in v7:
time: 89.4 us; the launch traced here: 88.9 us
  Pallas kernels  84.8 us (95%)
  local copies, waits for them, and re-layouts  3.5 us (4%)
    pallas_call x1, Pallas kernels, on_device(): pl.pallas_call(functools.partial(block_kernel, scale), out_shape=(sds((3,...  84.8 us
    unnamed x7, local copies, waits for them, and re-layouts  3.5 us

profile of v7, /device:TPU:4, one launch (start us, length us, event | category | flops | bytes accessed | tf_op | source)
XLA Modules:
  0.0 88.9 jit_solution(14695856219657747621)
XLA Ops:
  0.6 84.8 %hyena_block.1 = (bf16[3,2,2,32,512]{4,3,2,1,0:T(8,128)(2,1)}, f32[64,512]{1,0:T(8,128)}, f32[512,128]{1,0:T(8,128)}) custom-call(bf16[32,4096]{1,0:T(8,128)(2,1)} %x_ref.1, bf16[32,4096]{1,0:T(8,128)(2,1)} %g_ref.1, bf16[3,64,512]{2,1,0:T(8,128)(2,1)} %bitcast.5, bf16[64,512]{1,0:T(8,128)(2,1)} %w_ref.1, bf16[512,128]{1,0:T(8,128)(2,1)} %filt_ref.1), custom_call_target="tpu_custom_call" | custom-call | tf_op jit(solution)/shard_map/hyena_block/pallas_call | solution.py:613
  85.4 0.0 copy-start.1
  85.4 1.8 %copy.11 = bf16[128,3,512]{2,0,1:T(8,128)(2,1)} copy(bf16[128,3,512]{2,0,1:T(8,128)(2,1)} %bitcast.4) | data formatting | bytes 786432
  87.2 0.0 copy-done.1
  87.2 0.0 copy-start
  87.2 0.7 copy.12
  87.9 0.3 copy-done
  88.2 0.7 copy.13
Async XLA Ops:
  85.4 1.8 %copy-start.1 = (f32[64,512]{1,0:T(8,128)S(1)}, f32[64,512]{1,0:T(8,128)}, u32[]{:S(2)}) copy-start(f32[64,512]{1,0:T(8,128)} %get-tuple-element.13) | copy-start | bytes 393220
  87.2 1.0 %copy-start = (f32[512,128]{1,0:T(8,128)S(1)}, f32[512,128]{1,0:T(8,128)}, u32[]{:S(2)}) copy-start(f32[512,128]{1,0:T(8,128)} %get-tuple-element.14) | copy-start | bytes 786436
